TPU v7x, 256 devices: a whole 4x4x8 slice. The times are simulated.
256 devices in a mesh: patch: 32 (over y, x, core), sub: 8 (over z).
Axes of the slice: x: 4, y: 4, z: 8, core: 2. Of those that a mesh axis runs over, the one named last changes fastest.
Arguments:
- nodes: bfloat16 [32768, 512], P(('patch', 'sub')), may hold values from -6 to 6
- fine_edges: bfloat16 [196608, 512], P(('patch', 'sub')), may hold values from -6 to 6
- long_edges: bfloat16 [65536, 512], P(('patch', 'sub')), may hold values from -6 to 6
- fine_send: int32 [196608], P(('patch', 'sub')), may hold values from 0 to 447
- fine_recv: int32 [196608], P(('patch', 'sub')), may hold values from 0 to 127
- long_send: int32 [65536], P(('patch', 'sub')), may hold values from 0 to 2047, as said below
- long_recv: int32 [65536], P(('patch', 'sub')), may hold values from 0 to 7
- long_mask: int32 [65536], P(('patch', 'sub')), may hold values from 0 to 1, as said below
- sub_list: int32 [2048, 32], P(('patch', 'sub')), may hold values from 0 to 127
- patch_list: int32 [512, 32], P(('patch', 'sub')), may hold values from 0 to 127
- edge_w1: bfloat16 [1536, 512], replicated, may hold values from -0.15625 to 0.15625
- edge_w2: bfloat16 [512, 512], replicated, may hold values from -0.25 to 0.25
- node_w1: bfloat16 [1024, 512], replicated, may hold values from -0.1875 to 0.1875
- node_w2: bfloat16 [512, 512], replicated, may hold values from -0.25 to 0.25
- upstream_nodes: bfloat16 [32768, 512], P(('patch', 'sub')), may hold values from -6 to 6
- upstream_fine: bfloat16 [196608, 512], P(('patch', 'sub')), may hold values from -6 to 6
- upstream_long: bfloat16 [65536, 512], P(('patch', 'sub')), may hold values from -6 to 6
Outputs:
- new_nodes: bfloat16 [32768, 512], P(('patch', 'sub'))
- new_fine: bfloat16 [196608, 512], P(('patch', 'sub'))
- new_long: bfloat16 [65536, 512], P(('patch', 'sub'))
- grad_nodes: bfloat16 [32768, 512], P(('patch', 'sub'))
- grad_fine: bfloat16 [196608, 512], P(('patch', 'sub'))
- grad_long: bfloat16 [65536, 512], P(('patch', 'sub'))
- grad_edge_first: float32 [1536, 512], P('patch')
- grad_edge_second: float32 [512, 512], P('patch')
- grad_node_first: float32 [1024, 512], P('patch')
- grad_node_second: float32 [512, 512], P('patch')
Inputs may be any that keep to these rules, and one draw needn't show every extreme that they name: `long_mask`: within the 256 slots of one block the live long edges come first; some block has all slots live. `long_send`: any coarse node may send to any block.
All inputs are finite; a program needn't handle non-finite values.
Results may differ from a plain program's by a relative error of at most 0.03.
Values may be sent and summed in bfloat16 or wider, within the bound.
A program may use at most 128 MiB of HBM per device.

v0:
```python
import jax
import jax.numpy as jnp
from jax import lax
from jax.sharding import PartitionSpec as P

COARSE_DEV = 8


eps = 1e-05


def shifted(shard, axis, by):
    peers = lax.axis_size(axis)
    return lax.ppermute(shard, axis, [(i, (i + by) % peers) for i in range(peers)])


def silu_slope(values):
    sigma = jax.nn.sigmoid(values)
    return sigma + values * sigma * (1.0 - sigma)


def norm_rows(values):
    row_mean = jnp.mean(values, axis=-1, keepdims=True)
    centered = values - row_mean
    inverse = lax.rsqrt(jnp.mean(centered * centered, axis=-1, keepdims=True) + eps)
    return (centered * inverse, inverse)


def norm_back(normed, inverse, upstream):
    mean_grad = jnp.mean(upstream, axis=-1, keepdims=True)
    mean_prod = jnp.mean(upstream * normed, axis=-1, keepdims=True)
    return (upstream - mean_grad - normed * mean_prod) * inverse


def contract(left, right):
    return lax.dot_general(
        left, right, (((0,), (0,)), ((), ())), preferred_element_type=jnp.float32
    )


def layer_pass(
    nodes,
    edge_in,
    recv_all,
    live_all,
    edge_w1,
    edge_w2,
    node_w1,
    node_w2,
    upstream_nodes,
    upstream_edges,
):
    features = nodes.shape[1]
    node_count = nodes.shape[0]
    edge_first = jnp.dot(edge_in, edge_w1, preferred_element_type=jnp.float32)
    edge_active = jax.nn.silu(edge_first).astype(jnp.bfloat16)
    edge_second = jnp.dot(edge_active, edge_w2, preferred_element_type=jnp.float32)
    edge_normed, edge_inverse = norm_rows(edge_second)
    new_edges = (edge_in[:, :features].astype(jnp.float32) + live_all * edge_normed).astype(
        jnp.bfloat16
    )
    aggregate = jax.ops.segment_sum(
        live_all * new_edges.astype(jnp.float32), recv_all, num_segments=node_count
    )
    aggregate = aggregate.astype(jnp.bfloat16)
    node_in = jnp.concatenate([nodes, aggregate], axis=1)
    node_first = jnp.dot(node_in, node_w1, preferred_element_type=jnp.float32)
    node_active = jax.nn.silu(node_first).astype(jnp.bfloat16)
    node_second = jnp.dot(node_active, node_w2, preferred_element_type=jnp.float32)
    node_normed, node_inverse = norm_rows(node_second)
    new_nodes = (nodes.astype(jnp.float32) + node_normed).astype(jnp.bfloat16)
    upstream_node_rows = upstream_nodes.astype(jnp.float32)
    node_grad_second = norm_back(node_normed, node_inverse, upstream_node_rows).astype(jnp.bfloat16)
    grad_node_second = contract(node_active, node_grad_second)
    node_grad_first = jnp.dot(
        node_grad_second, node_w2.T, preferred_element_type=jnp.float32
    ) * silu_slope(node_first)
    node_grad_first = node_grad_first.astype(jnp.bfloat16)
    grad_node_first = contract(node_in, node_grad_first)
    node_grad_in = jnp.dot(node_grad_first, node_w1.T, preferred_element_type=jnp.float32)
    grad_aggregate = node_grad_in[:, features:]
    edge_grad_new = upstream_edges.astype(jnp.float32) + live_all * jnp.take(
        grad_aggregate, recv_all, axis=0
    )
    edge_grad_second = (live_all * norm_back(edge_normed, edge_inverse, edge_grad_new)).astype(
        jnp.bfloat16
    )
    grad_edge_second = contract(edge_active, edge_grad_second)
    edge_grad_first = jnp.dot(
        edge_grad_second, edge_w2.T, preferred_element_type=jnp.float32
    ) * silu_slope(edge_first)
    edge_grad_first = edge_grad_first.astype(jnp.bfloat16)
    grad_edge_first = contract(edge_in, edge_grad_first)
    edge_grad_in = jnp.dot(edge_grad_first, edge_w1.T, preferred_element_type=jnp.float32)
    grad_edges = (edge_grad_new + edge_grad_in[:, :features]).astype(jnp.bfloat16)
    grad_local = upstream_node_rows + node_grad_in[:, :features]
    grad_local = grad_local + jax.ops.segment_sum(
        edge_grad_in[:, 2 * features :], recv_all, num_segments=node_count
    )
    sender_grad = edge_grad_in[:, features : 2 * features]
    weight_terms = (grad_edge_first, grad_edge_second, grad_node_first, grad_node_second)
    return (new_nodes, new_edges, grad_local, grad_edges, sender_grad, weight_terms)


def per_device(
    nodes,
    fine_edges,
    long_edges,
    fine_send,
    fine_recv,
    long_send,
    long_recv,
    long_mask,
    sub_list,
    patch_list,
    edge_w1,
    edge_w2,
    node_w1,
    node_w2,
    upstream_nodes,
    upstream_fine,
    upstream_long,
):
    features = nodes.shape[1]
    node_count = nodes.shape[0]
    fine_count = fine_edges.shape[0]
    blocks_sub = lax.axis_size("sub")
    list_rows = sub_list.shape[1]
    group_nodes = lax.all_gather(nodes, "sub", axis=0, tiled=True)
    group_lists = lax.all_gather(sub_list, "sub", axis=0, tiled=True)
    picked_rows = lax.dynamic_index_in_dim(
        group_lists.reshape(blocks_sub, blocks_sub, list_rows),
        lax.axis_index("sub"),
        1,
        keepdims=False,
    )
    offsets = jnp.arange(blocks_sub, dtype=jnp.int32) * node_count
    group_index = (picked_rows + offsets[:, None]).reshape(-1)
    sub_rows = jnp.take(group_nodes, group_index, axis=0)
    from_lower = shifted(jnp.take(nodes, patch_list[0], axis=0), "patch", 1)
    from_upper = shifted(jnp.take(nodes, patch_list[1], axis=0), "patch", -1)
    extended = jnp.concatenate([nodes, sub_rows, from_lower, from_upper], axis=0)
    coarse_all = lax.all_gather(nodes[:COARSE_DEV], ("patch", "sub"), axis=0, tiled=True)
    receivers = jnp.concatenate([fine_recv, long_recv])
    edge_in = jnp.concatenate(
        [
            jnp.concatenate([fine_edges, long_edges], axis=0),
            jnp.concatenate(
                [jnp.take(extended, fine_send, axis=0), jnp.take(coarse_all, long_send, axis=0)],
                axis=0,
            ),
            jnp.take(nodes, receivers, axis=0),
        ],
        axis=1,
    )
    live_all = jnp.concatenate(
        [jnp.ones((fine_count, 1), jnp.float32), long_mask.astype(jnp.float32)[:, None]], axis=0
    )
    upstream_edges = jnp.concatenate([upstream_fine, upstream_long], axis=0)
    new_nodes, new_edges, grad_local, grad_edges, sender_grad, weight_terms = layer_pass(
        nodes,
        edge_in,
        receivers,
        live_all,
        edge_w1,
        edge_w2,
        node_w1,
        node_w2,
        upstream_nodes,
        upstream_edges,
    )
    ext_grad = jax.ops.segment_sum(
        sender_grad[:fine_count], fine_send, num_segments=extended.shape[0]
    )
    halo_start = node_count + blocks_sub * list_rows
    sub_grad = ext_grad[node_count:halo_start]
    lower_grad = ext_grad[halo_start : halo_start + list_rows]
    upper_grad = ext_grad[halo_start + list_rows :]
    group_table = jax.ops.segment_sum(sub_grad, group_index, num_segments=blocks_sub * node_count)
    returned = lax.psum_scatter(
        group_table.astype(jnp.bfloat16), "sub", scatter_dimension=0, tiled=True
    ).astype(jnp.float32)
    back_lower = shifted(lower_grad.astype(jnp.bfloat16), "patch", -1).astype(lower_grad.dtype)
    back_upper = shifted(upper_grad.astype(jnp.bfloat16), "patch", 1).astype(upper_grad.dtype)
    patch_back = jax.ops.segment_sum(back_lower, patch_list[0], num_segments=node_count)
    patch_back = patch_back + jax.ops.segment_sum(
        back_upper, patch_list[1], num_segments=node_count
    )
    coarse_total = COARSE_DEV * lax.axis_size("patch") * lax.axis_size("sub")
    coarse_table = jax.ops.segment_sum(
        sender_grad[fine_count:], long_send, num_segments=coarse_total
    )
    coarse_back = lax.psum_scatter(coarse_table, ("patch", "sub"), scatter_dimension=0, tiled=True)
    coarse_full = jnp.concatenate(
        [coarse_back, jnp.zeros((node_count - COARSE_DEV, features), jnp.float32)], axis=0
    )
    grad_nodes = (grad_local + ext_grad[:node_count] + returned + patch_back + coarse_full).astype(
        jnp.bfloat16
    )
    shares = (
        lax.psum_scatter(
            weight_terms[0].astype(jnp.bfloat16), "patch", scatter_dimension=0, tiled=True
        ).astype(jnp.float32),
        lax.psum_scatter(
            weight_terms[1].astype(jnp.bfloat16), "patch", scatter_dimension=0, tiled=True
        ).astype(jnp.float32),
        lax.psum_scatter(
            weight_terms[2].astype(jnp.bfloat16), "patch", scatter_dimension=0, tiled=True
        ).astype(jnp.float32),
        lax.psum_scatter(
            weight_terms[3].astype(jnp.bfloat16), "patch", scatter_dimension=0, tiled=True
        ).astype(jnp.float32),
    )
    totals = (
        lax.psum(shares[0].astype(jnp.bfloat16), "sub").astype(jnp.float32),
        lax.psum(shares[1].astype(jnp.bfloat16), "sub").astype(jnp.float32),
        lax.psum(shares[2].astype(jnp.bfloat16), "sub").astype(jnp.float32),
        lax.psum(shares[3].astype(jnp.bfloat16), "sub").astype(jnp.float32),
    )
    return (
        new_nodes,
        new_edges[:fine_count],
        new_edges[fine_count:],
        grad_nodes,
        grad_edges[:fine_count],
        grad_edges[fine_count:],
        totals[0],
        totals[1],
        totals[2],
        totals[3],
    )


def solution(mesh):
    placed = (
        P(("patch", "sub"), None),
        P(("patch", "sub"), None),
        P(("patch", "sub"), None),
        P(("patch", "sub")),
        P(("patch", "sub")),
        P(("patch", "sub")),
        P(("patch", "sub")),
        P(("patch", "sub")),
        P(("patch", "sub"), None),
        P(("patch", "sub"), None),
        P(),
        P(),
        P(),
        P(),
        P(("patch", "sub"), None),
        P(("patch", "sub"), None),
        P(("patch", "sub"), None),
    )
    return jax.shard_map(
        per_device,
        mesh=mesh,
        in_specs=placed,
        out_specs=(
            P(("patch", "sub"), None),
            P(("patch", "sub"), None),
            P(("patch", "sub"), None),
            P(("patch", "sub"), None),
            P(("patch", "sub"), None),
            P(("patch", "sub"), None),
            P("patch", None),
            P("patch", None),
            P("patch", None),
            P("patch", None),
        ),
        check_vma=False,
    )
```

profile of v0, /device:TPU:32, one launch (start us, length us, event | category | flops | bytes accessed | tf_op | source)
XLA Modules:
  0.0 1932.5 jit_solution(15210802734070192143)
XLA Ops:
  14.9 5.1 collective-permute-start.1
  23.0 27.9 %all_gather.9 = s32[64,32]{1,0:T(8,128)S(1)} all-gather(s32[8,32]{1,0:T(8,128)} %param.27), channel_id=1, replica_groups=mesh['patch'=32,'sub'=8] {'sub'}, dimensions={0}, use_global_device_ids=true | all-gather | bytes 9216 | tf_op jit(solution)/shard_map/all_gather | solution.py:130
  54.8 4.0 gather_fusion.3
  74.7 2.3 broadcast_select_fusion
  77.0 2.6 gather_fusion
  83.0 3.3 gather_fusion.1
  88.7 68.9 %all-gather.5.cloned.1.call-done = bf16[2048,512]{1,0:T(8,128)(2,1)} async-done(((bf16[8,512]{1,0:T(8,128)(2,1)}), bf16[2048,512]{1,0:T(8,128)(2,1)}) %all-gather.5.cloned.1.call-update) | async-done | bytes 2097168 | tf_op jit(solution)/shard_map/all_gather | solution.py:143
  157.6 3.9 gather_fusion.2
  164.3 5.0 fusion.7
  172.6 3.0 copy.55
  175.6 7.5 scatter_custom_fusion
  192.7 4.9 gather_fusion.4
  197.6 2.9 copy.58
  200.5 3.1 fusion.39
  209.1 3.5 multiply_convert_fusion
  213.6 11.8 convolution_convert_fusion
  225.7 5.7 fusion.45
  231.4 7.6 scatter_custom_fusion.1
  239.0 3.7 scatter_custom_fusion.2
  242.8 2.7 convert_element_type.108
  245.5 28.8 %reduce-scatter.17.cloned.1.call-done = bf16[16,512]{1,0:T(8,128)(2,1)} async-done(((bf16[512,512]{1,0:T(8,128)(2,1)}), bf16[16,512]{1,0:T(8,128)(2,1)}) %reduce-scatter.17.cloned.1.call-update) | async-done | bytes 16400 | tf_op jit(solution)/shard_map/reduce_scatter | solution.py:210
  274.3 87.6 %reduce-scatter.13.cloned.1.call-done = bf16[16,512]{1,0:T(8,128)(2,1)} async-done(((bf16[512,512]{1,0:T(8,128)(2,1)}), bf16[16,512]{1,0:T(8,128)(2,1)}) %reduce-scatter.13.cloned.1.call-update) | async-done | bytes 16400 | tf_op jit(solution)/shard_map/reduce_scatter | solution.py:204
  362.0 88.2 %reduce-scatter.15.cloned.1.call-done = bf16[32,512]{1,0:T(8,128)(2,1)} async-done(((bf16[1024,512]{1,0:T(8,128)(2,1)}), bf16[32,512]{1,0:T(8,128)(2,1)}) %reduce-scatter.15.cloned.1.call-update) | async-done | bytes 32784 | tf_op jit(solution)/shard_map/reduce_scatter | solution.py:207
  450.1 89.4 %reduce-scatter.11.cloned.1.call-done = bf16[48,512]{1,0:T(8,128)(2,1)} async-done(((bf16[1536,512]{1,0:T(8,128)(2,1)}), bf16[48,512]{1,0:T(8,128)(2,1)}) %reduce-scatter.11.cloned.1.call-update) | async-done | bytes 49168 | tf_op jit(solution)/shard_map/reduce_scatter | solution.py:201
  539.6 4.9 scatter_custom_fusion.5
  545.3 3.1 slice.100
  549.1 2.9 copy.64
  554.2 2.8 add_convert_fusion
  566.8 12.9 reduce-scatter.7.cloned.1.call-done
  580.8 7.5 scatter_custom_fusion.3
  588.3 65.5 %all-reduce.5.cloned.1.call-done = (bf16[48,512]{1,0:T(8,128)(2,1)}, bf16[16,512]{1,0:T(8,128)(2,1)}, bf16[32,512]{1,0:T(8,128)(2,1)}, bf16[16,512]{1,0:T(8,128)(2,1)}) async-done(((bf16[48,512]{1,0:T(8,128)(2,1)}, bf16[16,512]{1,0:T(8,128)(2,1)}, bf16[32,512]{1,0:T(8,128)(2,1)}, bf16[16,512]{1,0:T(8,128)(2,1)}), (bf16[48,512]{1,0:T(8,128)(2,1)}, bf16[16,512]{1,0:T(8,128)(2,1)}, bf16[32,512]{1,0:T(8,128)(2,1)}, ...) | async-done | bytes 114704 | tf_op jit(solution)/shard_map/psum | solution.py:215
  659.3 1264.9 %reduce-scatter.9.cloned.1.call-done = f32[8,512]{1,0:T(8,128)} async-done(((f32[2048,512]{1,0:T(8,128)}), f32[8,512]{1,0:T(8,128)}) %reduce-scatter.9.cloned.1.call-update) | async-done | bytes 16400 | tf_op jit(solution)/shard_map/reduce_scatter | solution.py:193
  (205 shorter events, 79.7 us)
Async XLA Ops:
  7.2 157.1 %copy-start = (bf16[1536,512]{1,0:T(8,128)(2,1)S(1)}, bf16[1536,512]{1,0:T(8,128)(2,1)}, u32[]{:S(2)}) copy-start(bf16[1536,512]{1,0:T(8,128)(2,1)} %param.29) | copy-start | bytes 4718596
  7.2 47.6 %copy-start.1 = (bf16[128,512]{1,0:T(8,128)(2,1)S(1)}, bf16[128,512]{1,0:T(8,128)(2,1)}, u32[]{:S(2)}) copy-start(bf16[128,512]{1,0:T(8,128)(2,1)} %param.19) | copy-start | bytes 393220
  7.2 69.8 %all-gather.3.cloned.1.call-start = ((), (), s32[]{:S(2)}) async-start(), calls=%async_computation.6 | async-start | bytes 1179648 | tf_op jit(solution)/shard_map/all_gather | solution.py:129
  7.9 149.7 %all-gather.5.cloned.1.call-start = ((), (), s32[]{:S(2)}) async-start(), calls=%async_computation.7 | async-start | bytes 2105344 | tf_op jit(solution)/shard_map/all_gather | solution.py:143
  9.3 265.0 %reduce-scatter.17.cloned.1.call-start = ((), (), s32[]{:S(2)}) async-start(), calls=%async_computation.13 | async-start | bytes 540672 | tf_op jit(solution)/shard_map/reduce_scatter | solution.py:210
  12.5 67.3 %collective-permute-start = (bf16[32,512]{0,1:T(8,128)(2,1)}, bf16[32,512]{0,1:T(8,128)(2,1)}, u32[]{:S(2)}, u32[]{:S(2)}) collective-permute-start(bf16[32,512]{0,1:T(8,128)(2,1)} %broadcast_select_fusion.5), channel_id=1, source_target_pairs={{0,8},{8,16},{16,24},{24,32},{32,40},{40,48},{48,56},{56,64},{64,7... | collective-permute-start | bytes 98312 | tf_op jit(solution)/shard_map/ppermute | solution.py:14
  14.9 65.0 %collective-permute-start.1 = (bf16[32,512]{0,1:T(8,128)(2,1)}, bf16[32,512]{0,1:T(8,128)(2,1)}, u32[]{:S(2)}, u32[]{:S(2)}) collective-permute-start(bf16[32,512]{0,1:T(8,128)(2,1)} %broadcast_select_fusion.4), channel_id=1, source_target_pairs={{0,248},{8,0},{16,8},{24,16},{32,24},{40,32},{48,40},{56,48},{64,5... | collective-permute-start | bytes 98312 | tf_op jit(solution)/shard_map/ppermute | solution.py:14
  60.1 5.6 copy-start.32
  60.1 9.4 copy-start.33
  74.7 4.9 copy-start.30
  83.0 4.7 copy-start.35
  87.7 75.6 %copy-start.38 = (pred[256]{0:T(512)(128)(4,1)S(1)}, pred[256]{0:T(512)(128)(4,1)}, u32[]{:S(2)}) copy-start(pred[256]{0:T(512)(128)(4,1)} %compare_and_fusion.4) | copy-start | bytes 772
  88.7 75.6 %copy-start.7 = (bf16[768,512]{0,1:T(8,128)(2,1)S(1)}, bf16[768,512]{0,1:T(8,128)(2,1)}, u32[]{:S(2)}) copy-start(bf16[768,512]{0,1:T(8,128)(2,1)} %copy.45) | copy-start | bytes 2359300
  164.3 5.0 copy-start.28
  164.3 5.0 copy-start.24
  175.6 10.7 copy-start.25
  183.2 5.7 copy-start.11
  190.3 171.6 %reduce-scatter.13.cloned.1.call-start = ((), (), s32[]{:S(2)}) async-start(), calls=%async_computation.11 | async-start | bytes 540672 | tf_op jit(solution)/shard_map/reduce_scatter | solution.py:204
  192.7 5.0 copy-start.9
  207.5 242.7 %reduce-scatter.15.cloned.1.call-start = ((), (), s32[]{:S(2)}) async-start(), calls=%async_computation.12 | async-start | bytes 1081344 | tf_op jit(solution)/shard_map/reduce_scatter | solution.py:207
  209.0 330.5 %reduce-scatter.11.cloned.1.call-start = ((), (), s32[]{:S(2)}) async-start(), calls=%async_computation.10 | async-start | bytes 1622016 | tf_op jit(solution)/shard_map/reduce_scatter | solution.py:201
  209.1 4.5 copy-start.8
  209.1 4.5 copy-start.14
  209.1 4.5 copy-start.19
  209.1 4.5 copy-start.22
  209.1 4.5 copy-start.29
  225.5 354.3 %reduce-scatter.7.cloned.1.call-start = ((), (), s32[]{:S(2)}) async-start(), calls=%async_computation.8 | async-start | bytes 1179648 | tf_op jit(solution)/shard_map/reduce_scatter | solution.py:180
  245.5 408.3 %all-reduce.5.cloned.1.call-start = ((), (), s32[]{:S(2)}) async-start(), calls=%async_computation.14 | async-start | bytes 229376 | tf_op jit(solution)/shard_map/psum | solution.py:215
  539.5 1384.7 %reduce-scatter.9.cloned.1.call-start = ((), (), s32[]{:S(2)}) async-start(), calls=%async_computation.9 | async-start | bytes 4210688 | tf_op jit(solution)/shard_map/reduce_scatter | solution.py:193
  553.4 12.1 collective-permute-start.2
  554.0 11.6 collective-permute-start.3
  561.5 18.2 copy-start.10
  (26 other events, 49.2 us)
Sparse Core Ops, SparseCore 0:
  9.8 40.6 all-gather.2
  54.8 102.7 all-gather.4
  190.4 83.8 reduce-scatter.16
  277.9 83.9 reduce-scatter.12
  365.6 84.4 reduce-scatter.14
  454.3 85.1 reduce-scatter.10
  542.2 37.4 reduce-scatter.6
  582.5 71.2 all-reduce.4
  656.3 1267.9 reduce-scatter.8
where the time goes:
time: 1940 us; the launch traced here: 1930 us
  waiting for transfers between devices  1710 us (88%)
  other arithmetic  70.2 us (4%)
  local copies, waits for them, and re-layouts  69 us (4%)
  matrix products  37 us (2%)
  blocking collectives  27.9 us (1%)
    reduce_scatter x1, waiting for transfers between devices, per_device(): lax.psum_scatter(coarse_table, ('patch', 'sub'), scatter_dimension=0, til...  1260 us
    reduce_scatter x1, waiting for transfers between devices, per_device(): lax.psum_scatter(weight_terms[0].astype(jnp.bfloat16), 'patch', scatter_d...  89.4 us
    reduce_scatter x1, waiting for transfers between devices, per_device(): lax.psum_scatter(weight_terms[2].astype(jnp.bfloat16), 'patch', scatter_d...  88.2 us
    reduce_scatter x1, waiting for transfers between devices, per_device(): lax.psum_scatter(weight_terms[1].astype(jnp.bfloat16), 'patch', scatter_d...  87.6 us
    all_gather x1, waiting for transfers between devices, per_device(): lax.all_gather(nodes[:COARSE_DEV], ('patch', 'sub'), axis=0, tiled=True)  68.9 us
    psum x1, waiting for transfers between devices, per_device(): lax.psum(shares[0].astype(jnp.bfloat16), 'sub').astype(jnp.float32)  65.5 us
  transfers between devices with their start and end apart: 13, of which 8 were waited for; matrix products, arithmetic and copies ran while one was open for 7% of the time, Pallas kernels for 0%

commit v1 on v0

v1 whole, which is shorter than its diff:
```python
import functools
import math

import jax
import jax.numpy as jnp
from jax import lax
from jax.experimental import pallas as pl
from jax.experimental.pallas import tpu as pltpu
from jax.sharding import PartitionSpec as P

COARSE_DEV = 8
F32 = jnp.float32
BF16 = jnp.bfloat16
MESH = pl.DeviceIdType.MESH
EPS = 1e-05
TILE = 256
VMEM_BYTES = 56 * 1024 * 1024


def dot(left, right):
    return jnp.dot(left, right, preferred_element_type=F32)


def dot_tn(left, right):
    return lax.dot_general(left, right, (((0,), (0,)), ((), ())), preferred_element_type=F32)


def dot_nt(left, right):
    return lax.dot_general(left, right, (((1,), (1,)), ((), ())), preferred_element_type=F32)


def split(values):
    high = values.astype(BF16)
    return high, (values - high.astype(F32)).astype(BF16)


def marks(hits):
    return jnp.where(hits, 1.0, 0.0).astype(BF16)


class Place:
    def __init__(self, side, depth):
        self.p = lax.axis_index("patch")
        self.z = lax.axis_index("sub")
        self.side, self.depth = side, depth
        self.core = lax.rem(self.p, 2)
        self.x = lax.rem(lax.div(self.p, 2), side)
        self.y = lax.div(self.p, 2 * side)
        self.patches = 2 * side * side

    def at(self, y, x, core):
        return (y * self.side + x) * 2 + core

    def along_x(self, by):
        return (self.at(self.y, lax.rem(self.x + by, self.side), self.core), self.z)

    def along_y(self, by):
        return (self.at(lax.rem(self.y + by, self.side), self.x, self.core), self.z)

    def along_z(self, by):
        return (self.p, lax.rem(self.z + by, self.depth))

    def other_core(self):
        return (self.at(self.y, self.x, 1 - self.core), self.z)

    def next_patch(self):
        return (lax.rem(self.p + 1, self.patches), self.z)

    def previous_patch(self):
        return (lax.rem(self.p + self.patches - 1, self.patches), self.z)

    def greet(self):
        peers = [self.along_x(by) for by in range(1, self.side)]
        peers += [self.along_y(by) for by in range(1, self.side)]
        peers += [self.along_z(by) for by in range(1, self.depth)]
        peers += [self.other_core(), self.next_patch(), self.previous_patch()]
        barrier = pltpu.get_barrier_semaphore()
        for peer in peers:
            pl.semaphore_signal(barrier, inc=1, device_id=peer, device_id_type=MESH)
        pl.semaphore_wait(barrier, len(peers))


def send(source, target, sent, landed, peer):
    copy = pltpu.make_async_remote_copy(
        src_ref=source,
        dst_ref=target,
        send_sem=sent,
        recv_sem=landed,
        device_id=peer,
        device_id_type=MESH,
    )
    copy.start()
    return copy


def gather_kernel(
    side, depth, nodes, lists, ext, low, high, rows, sub_s, sub_r, pat_s, pat_r, z_s, z_r, a_s, a_r, b_s, b_r, c_s, c_r
):
    me = Place(side, depth)
    count, width = nodes.shape
    half = depth // 2
    hb = (lists.shape[1]) // (depth + 2)
    first = nodes[0:16, :].astype(F32)[0:8, :]
    block = jnp.concatenate([first[:, : width // 2], first[:, width // 2 :]], axis=0).astype(BF16)

    in_low = me.z < half
    z_low = lax.rem(me.z, half)

    @pl.when(in_low)
    def _():
        low[me.core, me.y, me.x, z_low] = block

    @pl.when(jnp.logical_not(in_low))
    def _():
        high[me.core, me.x, me.y, z_low] = block

    picks = marks(lax.broadcasted_iota(jnp.int32, (count, lists.shape[1]), 0) == lists[...])
    rows[...] = dot_tn(picks, nodes[...]).astype(BF16).reshape(depth + 2, hb, width)

    me.greet()

    def z_copy(by):
        mine_low = low.at[me.core, me.y, me.x, z_low]
        mine_high = high.at[me.core, me.x, me.y, z_low]
        peer = me.along_z(by)

        @pl.when(in_low)
        def _():
            send(mine_low, mine_low, z_s.at[by - 1], z_r.at[by - 1], peer)

        @pl.when(jnp.logical_not(in_low))
        def _():
            send(mine_high, mine_high, z_s.at[by - 1], z_r.at[by - 1], peer)

    for by in range(1, depth):
        z_copy(by)
    halo = []
    for by in range(1, depth):
        peer = me.along_z(by)
        target = ext.at[pl.ds(pl.multiple_of(count + hb * me.z, hb), hb), :]
        halo.append(send(rows.at[peer[1]], target, sub_s.at[by - 1], sub_r.at[by - 1], peer))
    lower = ext.at[pl.ds(count + hb * depth, hb), :]
    upper = ext.at[pl.ds(count + hb * (depth + 1), hb), :]
    halo.append(send(rows.at[depth], lower, pat_s.at[0], pat_r.at[0], me.next_patch()))
    halo.append(send(rows.at[depth + 1], upper, pat_s.at[1], pat_r.at[1], me.previous_patch()))
    ext[0:count, :] = nodes[...]
    ext[pl.ds(pl.multiple_of(count + hb * me.z, hb), hb), :] = rows[me.z]

    mine = low.at[0, 0, 0, 0]
    for by in range(1, depth):
        pltpu.make_async_remote_copy(
            src_ref=mine,
            dst_ref=mine,
            send_sem=z_s.at[by - 1],
            recv_sem=z_r.at[by - 1],
            device_id=me.along_z(by),
            device_id_type=MESH,
        ).wait()

    low_one = low.at[me.core, me.y, me.x]
    high_one = high.at[me.core, me.x, me.y]
    stage = []
    for by in range(1, side):
        stage.append(send(low_one, low_one, a_s.at[0, by - 1], a_r.at[0, by - 1], me.along_x(by)))
        stage.append(send(high_one, high_one, b_s.at[0, by - 1], b_r.at[0, by - 1], me.along_y(by)))
    for copy in stage:
        copy.wait()
    low_row = low.at[me.core, me.y]
    high_row = high.at[me.core, me.x]
    stage = []
    for by in range(1, side):
        stage.append(send(low_row, low_row, a_s.at[1, by - 1], a_r.at[1, by - 1], me.along_y(by)))
        stage.append(send(high_row, high_row, b_s.at[1, by - 1], b_r.at[1, by - 1], me.along_x(by)))
    for copy in stage:
        copy.wait()
    low_all, high_all = low.at[me.core], high.at[me.core]
    last = [
        send(low_all, low_all, c_s.at[0], c_r.at[0], me.other_core()),
        send(high_all, high_all, c_s.at[1], c_r.at[1], me.other_core()),
    ]
    for copy in halo + last:
        copy.wait()


def gather_rows(side, depth, nodes, lists):
    count, width = nodes.shape
    hb = lists.shape[1] // (depth + 2)
    half = depth // 2
    whole = pl.BlockSpec(memory_space=pltpu.VMEM)
    sem = pltpu.SemaphoreType.DMA
    table = jax.ShapeDtypeStruct((2, side, side, half, 16, width // 2), BF16)
    return pl.pallas_call(
        functools.partial(gather_kernel, side, depth),
        out_shape=(jax.ShapeDtypeStruct((count + lists.shape[1], width), BF16), table, table),
        in_specs=[whole] * 2,
        out_specs=(whole,) * 3,
        scratch_shapes=[
            pltpu.VMEM((depth + 2, hb, width), BF16),
            sem((depth - 1,)),
            sem((depth - 1,)),
            sem((2,)),
            sem((2,)),
            sem((depth - 1,)),
            sem((depth - 1,)),
            sem((2, side - 1)),
            sem((2, side - 1)),
            sem((2, side - 1)),
            sem((2, side - 1)),
            sem((2,)),
            sem((2,)),
        ],
        compiler_params=pltpu.CompilerParams(
            collective_id=0, has_side_effects=True, vmem_limit_bytes=VMEM_BYTES
        ),
        name="gather_rows",
    )(nodes, lists)


def norm_rows(values):
    centered = values - jnp.mean(values, axis=-1, keepdims=True)
    inverse = lax.rsqrt(jnp.mean(centered * centered, axis=-1, keepdims=True) + EPS)
    return centered * inverse, inverse


def norm_back(normed, inverse, upstream):
    mean_grad = jnp.mean(upstream, axis=-1, keepdims=True)
    mean_prod = jnp.mean(upstream * normed, axis=-1, keepdims=True)
    return (upstream - mean_grad - normed * mean_prod) * inverse


def silu_and_slope(values):
    sigma = 0.5 + 0.5 * jnp.tanh(0.5 * values)
    active = values * sigma
    return active, sigma + active * (1.0 - sigma)


def layer_kernel(
    side,
    depth,
    nodes,
    fine,
    longs,
    ext,
    low,
    high,
    idx,
    w1,
    w2,
    nw1,
    nw2,
    up_nodes,
    up_fine,
    up_long,
    new_nodes,
    new_fine,
    new_long,
    grad_fine,
    grad_long,
    table,
    halo,
    own,
    local,
    cols,
    slope,
    active,
    normed,
    inverse,
    senders,
    recv_proj,
    agg,
    ga,
    g1,
    g2,
    g_recv,
    g_ext,
    egf_long,
):
    count, width = nodes.shape
    fine_count = fine.shape[0]
    long_count = longs.shape[0]
    ext_rows = ext.shape[0]
    patches = 2 * side * side
    fine_tiles = fine_count // TILE
    long_tile = fine_count

    cols[...] = idx[...].T
    for ref in (agg, g1, g2, g_recv, g_ext):
        ref[...] = jnp.zeros_like(ref)

    high_part, low_part = split(dot(nodes[...], w1[2 * width : 3 * width, :]))
    recv_proj[0:count, :] = high_part
    recv_proj[count : 2 * count, :] = low_part

    def recv_cols(base):
        lanes = lax.broadcasted_iota(jnp.int32, (TILE, 2 * count), 1)
        return marks(lax.rem(lanes, count) == cols[pl.ds(base, TILE), 1:2])

    def recv_rows(base, live):
        rows = lax.broadcasted_iota(jnp.int32, (count, TILE), 0)
        hits = rows == idx[1:2, pl.ds(base, TILE)]
        if live:
            hits = jnp.logical_and(hits, idx[2:3, pl.ds(base, TILE)] > 0)
        return marks(hits)

    def forward(base, edges, sender, live):
        senders[pl.ds(base, TILE), :] = sender
        first = (
            dot(edges, w1[0:width, :])
            + dot(sender, w1[width : 2 * width, :])
            + dot(recv_cols(base), recv_proj[...])
        )
        act, slopes = silu_and_slope(first)
        act = act.astype(BF16)
        slope[pl.ds(base, TILE), :] = slopes
        active[pl.ds(base, TILE), :] = act
        unit, scale = norm_rows(dot(act, w2[...]))
        normed[pl.ds(base, TILE), :] = unit
        inverse[pl.ds(base, TILE), :] = jnp.broadcast_to(scale, (TILE, 128))
        if live is not None:
            unit = unit * live
        new = (edges.astype(F32) + unit).astype(BF16)
        agg[...] += dot(recv_rows(base, live is not None), new)
        return new

    def fine_forward(step, carry):
        base = pl.multiple_of(step * TILE, TILE)
        picks = marks(
            lax.broadcasted_iota(jnp.int32, (TILE, ext_rows), 1) == cols[pl.ds(base, TILE), 0:1]
        )
        sender = dot(picks, ext[...]).astype(BF16)
        new_fine[pl.ds(base, TILE), :] = forward(base, fine[pl.ds(base, TILE), :], sender, None)
        return carry

    lax.fori_loop(0, fine_tiles, fine_forward, 0)

    spot = cols[long_tile : long_tile + long_count, 0:1]
    major_rows = math.prod(low.shape[2:-1])
    lanes = lax.broadcasted_iota(jnp.int32, (long_count, major_rows), 1)
    left = jnp.zeros((long_count, width // 2), F32)
    right = jnp.zeros((long_count, width // 2), F32)
    for number in range(4 * side):
        part = low if number < 2 * side else high
        piece = part[number // side % 2, number % side].reshape(major_rows, width // 2)
        shifted = spot - number * major_rows
        left += dot(marks(lanes == shifted), piece)
        right += dot(marks(lanes == shifted + 8), piece)
    sender = jnp.concatenate([left, right], axis=1).astype(BF16)
    live = cols[long_tile : long_tile + long_count, 2:3].astype(F32)
    new_long[...] = forward(long_tile, longs[...], sender, live)

    node_rows = nodes[...]
    aggregate = agg[...].astype(BF16)
    node_first = dot(node_rows, nw1[0:width, :]) + dot(aggregate, nw1[width : 2 * width, :])
    node_active, node_slope = silu_and_slope(node_first)
    node_active = node_active.astype(BF16)
    node_normed, node_inverse = norm_rows(dot(node_active, nw2[...]))
    new_nodes[...] = (node_rows.astype(F32) + node_normed).astype(BF16)
    upstream = up_nodes[...].astype(F32)
    ngs = norm_back(node_normed, node_inverse, upstream).astype(BF16)
    ngf = (dot_nt(ngs, nw2[...]) * node_slope).astype(BF16)

    coarse_rows = COARSE_DEV * depth
    per = [w1.shape[0] // patches, w2.shape[0] // patches, nw1.shape[0] // patches, nw2.shape[0] // patches]
    starts = [coarse_rows, coarse_rows + per[0], coarse_rows + per[0] + per[1], coarse_rows + sum(per[:3])]

    def put(patch, start, values):
        core, x, y = patch % 2, patch // 2 % side, patch // (2 * side)
        values = values.astype(BF16)
        rows = pl.ds(start, values.shape[0])
        table[core, 0, x, y, rows, :] = values[:, : width // 2]
        table[core, 1, y, x, rows, :] = values[:, width // 2 :]

    def put_all(kind, values, first_patch, patch_count):
        for k in range(patch_count):
            put(first_patch + k, starts[kind], values[k * per[kind] : (k + 1) * per[kind], :])

    put_all(3, dot_tn(node_active, ngs), 0, patches)
    put_all(2, dot_tn(node_rows, ngf), 0, patches // 2)
    put_all(2, dot_tn(aggregate, ngf), patches // 2, patches // 2)
    local[...] = upstream + dot_nt(ngf, nw1[0:width, :])
    high_part, low_part = split(dot_nt(ngf, nw1[width : 2 * width, :]))
    ga[0:count, :] = high_part
    ga[count : 2 * count, :] = low_part

    def backward(base, edges, upstream_rows, live):
        pulled = dot(recv_cols(base), ga[...])
        if live is not None:
            pulled = pulled * live
        egn = upstream_rows.astype(F32) + pulled
        egs = norm_back(normed[pl.ds(base, TILE), :], inverse[pl.ds(base, TILE), 0:1], egn)
        if live is not None:
            egs = egs * live
        egs = egs.astype(BF16)
        egf = (dot_nt(egs, w2[...]) * slope[pl.ds(base, TILE), :]).astype(BF16)
        g2[...] += dot_tn(active[pl.ds(base, TILE), :], egs)
        g1[0:width, :] += dot_tn(edges, egf)
        g1[width : 2 * width, :] += dot_tn(senders[pl.ds(base, TILE), :], egf)
        g_recv[...] += dot(recv_rows(base, False), egf)
        return egf, (egn + dot_nt(egf, w1[0:width, :])).astype(BF16)

    def fine_backward(step, carry):
        base = pl.multiple_of(step * TILE, TILE)
        egf, grad = backward(base, fine[pl.ds(base, TILE), :], up_fine[pl.ds(base, TILE), :], None)
        grad_fine[pl.ds(base, TILE), :] = grad
        rows = lax.broadcasted_iota(jnp.int32, (ext_rows, TILE), 0)
        g_ext[...] += dot(marks(rows == idx[0:1, pl.ds(base, TILE)]), egf)
        return carry

    egf, grad = backward(long_tile, longs[...], up_long[...], live)
    grad_long[...] = grad
    egf_long[...] = egf
    lax.fori_loop(0, fine_tiles, fine_backward, 0)

    sources = idx[3:4, long_tile : long_tile + long_count]
    for patch in range(0, patches, 4):
        rows = lax.broadcasted_iota(jnp.int32, (4 * coarse_rows, long_count), 0) + patch * coarse_rows
        sums = dot(marks(rows == sources), egf_long[...])
        for k in range(4):
            put(patch + k, 0, sums[k * coarse_rows : (k + 1) * coarse_rows, :])

    high_part, low_part = split(g_recv[...])
    g1[2 * width : 3 * width, :] = dot_tn(node_rows, high_part) + dot_tn(node_rows, low_part)
    receiver_w = w1[2 * width : 3 * width, :]
    local[...] += dot_nt(high_part, receiver_w) + dot_nt(low_part, receiver_w)
    for patch in range(patches):
        put(patch, starts[0], g1[patch * per[0] : (patch + 1) * per[0], :])
        put(patch, starts[1], g2[patch * per[1] : (patch + 1) * per[1], :])
    own[...] = g_ext[0:count, :]
    halo[...] = g_ext[count:ext_rows, :].astype(BF16)


def layer(side, depth, nodes, fine, longs, ext, low, high, idx, w1, w2, nw1, nw2, up_nodes, up_fine, up_long):
    count, width = nodes.shape
    edges = fine.shape[0] + longs.shape[0]
    patches = 2 * side * side
    chunk = COARSE_DEV * depth + (w1.shape[0] + w2.shape[0] + nw1.shape[0] + nw2.shape[0]) // patches
    whole = pl.BlockSpec(memory_space=pltpu.VMEM)

    def like(array):
        return jax.ShapeDtypeStruct(array.shape, array.dtype)

    def shape(dims, kind):
        return jax.ShapeDtypeStruct(dims, kind)

    return pl.pallas_call(
        functools.partial(layer_kernel, side, depth),
        out_shape=(
            like(nodes),
            like(fine),
            like(longs),
            like(fine),
            like(longs),
            shape((2, 2, side, side, chunk, width // 2), BF16),
            shape((ext.shape[0] - count, width), BF16),
            shape((count, width), F32),
            shape((count, width), F32),
        ),
        in_specs=[whole] * 14,
        out_specs=(whole,) * 9,
        scratch_shapes=[
            pltpu.VMEM((edges, idx.shape[0]), jnp.int32),
            pltpu.VMEM((edges, width), F32),
            pltpu.VMEM((edges, width), BF16),
            pltpu.VMEM((edges, width), F32),
            pltpu.VMEM((edges, 128), F32),
            pltpu.VMEM((edges, width), BF16),
            pltpu.VMEM((2 * count, width), BF16),
            pltpu.VMEM((count, width), F32),
            pltpu.VMEM((2 * count, width), BF16),
            pltpu.VMEM(w1.shape, F32),
            pltpu.VMEM(w2.shape, F32),
            pltpu.VMEM((count, width), F32),
            pltpu.VMEM((ext.shape[0], width), F32),
            pltpu.VMEM((longs.shape[0], width), BF16),
        ],
        compiler_params=pltpu.CompilerParams(vmem_limit_bytes=VMEM_BYTES),
        name="layer",
    )(nodes, fine, longs, ext, low, high, idx, w1, w2, nw1, nw2, up_nodes, up_fine, up_long)


def reduce_kernel(
    side,
    depth,
    table,
    halo,
    own,
    local,
    lists,
    w1,
    out_a,
    out_b,
    out_c,
    out_d,
    grad_nodes,
    mine,
    other,
    first_in,
    second,
    second_in,
    z_out,
    z_in,
    shares,
    back,
    local_sem,
    core_s,
    core_r,
    x_s,
    x_r,
    y_s,
    y_r,
    z_s,
    z_r,
    w_s,
    w_r,
    sub_s,
    sub_r,
    pat_s,
    pat_r,
):
    me = Place(side, depth)
    count, width = own.shape
    half = width // 2
    hb = lists.shape[1] // (depth + 2)
    coarse_rows = COARSE_DEV * depth
    chunk = table.shape[4]
    share = (z_out.shape[1] - 16) // 2
    order = [2, 1, 3, 0] if side == 4 else list(range(1, side)) + [0]
    majors = (me.x, me.y)
    minors = (me.y, me.x)

    locals_ = {}
    for by in order:
        for part in (0, 1):
            major = lax.rem(majors[part] + by, side)
            copy = pltpu.make_async_copy(
                table.at[me.core, part, major], mine.at[part, major], local_sem.at[part, by]
            )
            copy.start()
            locals_[part, by] = copy

    me.greet()

    cores = {}
    for by in order:
        for part in (0, 1):
            major = lax.rem(majors[part] + by, side)
            cores[part, by] = send(
                table.at[1 - me.core, part, major],
                other.at[part, major],
                core_s.at[part, by],
                core_r.at[part, by],
                me.other_core(),
            )

    returns = []
    for by in range(1, depth):
        peer = me.along_z(by)
        source = halo.at[pl.ds(pl.multiple_of(hb * peer[1], hb), hb), :]
        returns.append(send(source, back.at[me.z], sub_s.at[by - 1], sub_r.at[by - 1], peer))
    lower = halo.at[pl.ds(hb * depth, hb), :]
    upper = halo.at[pl.ds(hb * (depth + 1), hb), :]
    returns.append(send(lower, back.at[depth], pat_s.at[0], pat_r.at[0], me.previous_patch()))
    returns.append(send(upper, back.at[depth + 1], pat_s.at[1], pat_r.at[1], me.next_patch()))
    back[me.z] = halo[pl.ds(pl.multiple_of(hb * me.z, hb), hb), :]

    firsts = {}
    for by in order:
        for part in (0, 1):
            major = lax.rem(majors[part] + by, side)
            locals_[part, by].wait()
            cores[part, by].wait_recv()

            def add(minor, carry, part=part, major=major):
                mine[part, major, minor] = mine[part, major, minor] + other[part, major, minor]
                return carry

            lax.fori_loop(0, side, add, 0)
            if by:
                peer = me.along_x(by) if part == 0 else me.along_y(by)
                firsts[part, by] = send(
                    mine.at[part, major],
                    first_in.at[part, by - 1],
                    x_s.at[part, by - 1],
                    x_r.at[part, by - 1],
                    peer,
                )

    for copy in returns:
        copy.wait()
    picks = marks(lax.broadcasted_iota(jnp.int32, (count, lists.shape[1]), 0) == lists[...])
    sent = own[...] + dot(picks, back[...].reshape((depth + 2) * hb, width))

    for key in firsts:
        firsts[key].wait_recv()
    seconds = {}
    for by in order:
        for part in (0, 1):
            minor = lax.rem(minors[part] + by, side)
            total = mine[part, majors[part], minor].astype(F32)
            for k in range(side - 1):
                total = total + first_in[part, k, minor].astype(F32)
            second[part, minor] = total.astype(BF16)
            if by:
                peer = me.along_y(by) if part == 0 else me.along_x(by)
                seconds[part, by] = send(
                    second.at[part, minor],
                    second_in.at[part, by - 1],
                    y_s.at[part, by - 1],
                    y_r.at[part, by - 1],
                    peer,
                )
    sums = []
    for part in (0, 1):
        for by in range(1, side):
            seconds[part, by].wait_recv()
        total = second[part, minors[part]].astype(F32)
        for k in range(side - 1):
            total = total + second_in[part, k].astype(F32)
        sums.append(total)

    blocks = (chunk - coarse_rows) // 16
    for k in range(depth):
        rows = slice(k * COARSE_DEV, (k + 1) * COARSE_DEV)
        z_out[k, 0:16, :] = jnp.concatenate([sums[0][rows, :], sums[1][rows, :]], axis=0).astype(BF16)
        for j in range(share // 16):
            at = k * (share // 16) + j
            for part in (0, 1):
                target = pl.ds(16 + part * share + 16 * j, 16)
                if at < blocks:
                    start = coarse_rows + 16 * at
                    z_out[k, target, :] = sums[part][start : start + 16, :].astype(BF16)
                else:
                    z_out[k, target, :] = jnp.zeros((16, half), BF16)
    zs = []
    for by in range(1, depth):
        peer = me.along_z(by)
        zs.append(send(z_out.at[peer[1]], z_in.at[by - 1], z_s.at[by - 1], z_r.at[by - 1], peer))
    for copy in zs:
        copy.wait_recv()
    total = z_out[me.z].astype(F32)
    for k in range(depth - 1):
        total = total + z_in[k].astype(F32)
    shares[me.z] = total[16:, :].astype(BF16)
    ws = []
    for by in range(1, depth):
        ws.append(send(shares.at[me.z], shares.at[me.z], w_s.at[by - 1], w_r.at[by - 1], me.along_z(by)))

    coarse = jnp.concatenate([total[0:8, :], total[8:16, :]], axis=1)
    sent = jnp.concatenate([sent[0:8, :] + coarse, sent[8:, :]], axis=0)
    high_part, low_part = split(sent)
    sender_w = w1[width : 2 * width, :]
    grad_nodes[...] = (local[...] + dot_nt(high_part, sender_w) + dot_nt(low_part, sender_w)).astype(BF16)

    for copy in ws:
        copy.wait_recv()
    at = 0
    for out in (out_a, out_b, out_c, out_d):
        for row in range(0, out.shape[0], 16):
            k, j = at // (share // 16), at % (share // 16)
            for part in (0, 1):
                piece = shares[k, part * share + 16 * j : part * share + 16 * (j + 1), :]
                out[row : row + 16, part * half : (part + 1) * half] = piece.astype(F32)
            at += 1
    for key in cores:
        cores[key].wait_send()
    for key in firsts:
        firsts[key].wait_send()
    for key in seconds:
        seconds[key].wait_send()
    for copy in zs + ws:
        copy.wait_send()


def reduce_all(side, depth, table, halo, own, local, lists, w1, sizes):
    count, width = own.shape
    half = width // 2
    hb = lists.shape[1] // (depth + 2)
    chunk = table.shape[4]
    blocks = (chunk - COARSE_DEV * depth) // 16
    share = 16 * -(-blocks // depth)
    whole = pl.BlockSpec(memory_space=pltpu.VMEM)
    sem = pltpu.SemaphoreType.DMA
    return pl.pallas_call(
        functools.partial(reduce_kernel, side, depth),
        out_shape=tuple(jax.ShapeDtypeStruct((rows, width), F32) for rows in sizes)
        + (jax.ShapeDtypeStruct((count, width), BF16),),
        in_specs=[pl.BlockSpec(memory_space=pl.ANY)] + [whole] * 5,
        out_specs=(whole,) * 5,
        scratch_shapes=[
            pltpu.VMEM((2, side, side, chunk, half), BF16),
            pltpu.VMEM((2, side, side, chunk, half), BF16),
            pltpu.VMEM((2, side - 1, side, chunk, half), BF16),
            pltpu.VMEM((2, side, chunk, half), BF16),
            pltpu.VMEM((2, side - 1, chunk, half), BF16),
            pltpu.VMEM((depth, 16 + 2 * share, half), BF16),
            pltpu.VMEM((depth - 1, 16 + 2 * share, half), BF16),
            pltpu.VMEM((depth, 2 * share, half), BF16),
            pltpu.VMEM((depth + 2, hb, width), BF16),
            sem((2, side)),
            sem((2, side)),
            sem((2, side)),
            sem((2, side - 1)),
            sem((2, side - 1)),
            sem((2, side - 1)),
            sem((2, side - 1)),
            sem((depth - 1,)),
            sem((depth - 1,)),
            sem((depth - 1,)),
            sem((depth - 1,)),
            sem((depth - 1,)),
            sem((depth - 1,)),
            sem((2,)),
            sem((2,)),
        ],
        compiler_params=pltpu.CompilerParams(
            collective_id=1, has_side_effects=True, vmem_limit_bytes=VMEM_BYTES
        ),
        name="reduce_all",
    )(table, halo, own, local, lists, w1)


def coarse_spot(side, depth, coarse):
    block, row = coarse // COARSE_DEV, coarse % COARSE_DEV
    patch, z = block // depth, block % depth
    core, x, y = patch % 2, patch // 2 % side, patch // (2 * side)
    half = depth // 2
    lower = z < half
    major, minor = jnp.where(lower, y, x), jnp.where(lower, x, y)
    place = ((core * side + major) * side + minor) * half + z % half
    return 16 * (place + jnp.where(lower, 0, 2 * side * side * half)) + row


def per_device(
    side,
    depth,
    nodes,
    fine_edges,
    long_edges,
    fine_send,
    fine_recv,
    long_send,
    long_recv,
    long_mask,
    sub_list,
    patch_list,
    edge_w1,
    edge_w2,
    node_w1,
    node_w2,
    upstream_nodes,
    upstream_fine,
    upstream_long,
):
    patches = 2 * side * side
    lists = jnp.concatenate([sub_list.reshape(1, -1), patch_list.reshape(1, -1)], axis=1)
    ones = jnp.ones_like(fine_send)
    none = jnp.zeros_like(fine_send)
    idx = jnp.stack(
        [
            jnp.concatenate([fine_send, coarse_spot(side, depth, long_send)]),
            jnp.concatenate([fine_recv, long_recv]),
            jnp.concatenate([ones, long_mask]),
            jnp.concatenate([none, long_send]),
        ]
    )
    idx = jnp.concatenate([idx, jnp.zeros_like(idx)], axis=0)
    ext, low, high = gather_rows(side, depth, nodes, lists)
    new_nodes, new_fine, new_long, grad_fine, grad_long, table, halo, own, local = layer(
        side,
        depth,
        nodes,
        fine_edges,
        long_edges,
        ext,
        low,
        high,
        idx,
        edge_w1,
        edge_w2,
        node_w1,
        node_w2,
        upstream_nodes,
        upstream_fine,
        upstream_long,
    )
    sizes = [w.shape[0] // patches for w in (edge_w1, edge_w2, node_w1, node_w2)]
    totals = reduce_all(side, depth, table, halo, own, local, lists, edge_w1, sizes)
    return (new_nodes, new_fine, new_long, totals[4], grad_fine, grad_long) + tuple(totals[:4])


def solution(mesh):
    side = math.isqrt(mesh.shape["patch"] // 2)
    depth = mesh.shape["sub"]
    rows = P(("patch", "sub"), None)
    flat = P(("patch", "sub"))
    return jax.shard_map(
        functools.partial(per_device, side, depth),
        mesh=mesh,
        in_specs=(rows,) * 3 + (flat,) * 5 + (rows,) * 2 + (P(),) * 4 + (rows,) * 3,
        out_specs=(rows,) * 6 + (P("patch", None),) * 4,
        check_vma=False,
    )
```

time: 1940 us -> 115 us (0.06)
  waiting for transfers between devices: 1710 us -> 0 us
  Pallas kernels: 0 us -> 100 us
  other arithmetic: 70.2 us -> 2.12 us
  local copies, waits for them, and re-layouts: 69 us -> 10.9 us
  matrix products: 37 us -> 0 us
  blocking collectives: 27.9 us -> 0 us
    reduce_scatter x6 -> x0, waiting for transfers between devices: 1570 us -> none  [the longest x1 1260 us: per_device(): lax.psum_scatter(coarse_table, ('patch', 'sub'), scatter_dimension=0, til...]
    pallas_call x0 -> x3, Pallas kernels: none -> 100 us  [the longest x1 48.9 us: reduce_all(): pl.pallas_call(functools.partial(reduce_kernel, side, depth), out_shape=t...]
    all_gather x2 -> x0, waiting for transfers between devices: 68.9 us -> none  [the longest x1 68.9 us: per_device(): lax.all_gather(nodes[:COARSE_DEV], ('patch', 'sub'), axis=0, tiled=True)]
    psum x1 -> x0, waiting for transfers between devices: 65.5 us -> none  [per_device(): lax.psum(shares[0].astype(jnp.bfloat16), 'sub').astype(jnp.float32)]
    dot_general x12 -> x0, matrix products: 37 us -> none  [the longest x4 16.1 us: contract(): lax.dot_general(left, right, (((0,), (0,)), ((), ())), preferred_element_...]
    scatter-add x5 -> x0, other arithmetic: 31.3 us -> none  [the longest x1 7.6 us: per_device(): jax.ops.segment_sum(sender_grad[:fine_count], fine_send, num_segments=ext...]
    gather x14 -> x0, local copies, waits for them, and re-layouts: 29.6 us -> none  [the longest x2 7.82 us: layer_pass(): jnp.take(grad_aggregate, recv_all, axis=0)]
    all_gather x1 -> x0, blocking collectives: 27.9 us -> none  [per_device(): group_lists = lax.all_gather(sub_list, 'sub', axis=0, tiled=True)]
  transfers between devices with their start and end apart: 13 -> 0, of which waited for: 8 -> 0; matrix products, arithmetic and copies ran while one was open for 7% -> 0% of each run, Pallas kernels for 0% -> 0%
where the time goes in v1:
time: 115 us; the launch traced here: 114 us
  Pallas kernels  100 us (87%)
  local copies, waits for them, and re-layouts  10.9 us (9%)
  other arithmetic  2.12 us (2%)
    pallas_call x1, Pallas kernels, reduce_all(): pl.pallas_call(functools.partial(reduce_kernel, side, depth), out_shape=t...  48.9 us
    pallas_call x1, Pallas kernels, gather_rows(): pl.pallas_call(functools.partial(gather_kernel, side, depth), out_shape=(...  29.7 us
    pallas_call x1, Pallas kernels, layer(): pl.pallas_call(functools.partial(layer_kernel, side, depth), out_shape=(l...  21.9 us
    unnamed x8, local copies, waits for them, and re-layouts  7.34 us

profile of v1, /device:TPU:32, one launch (start us, length us, event | category | flops | bytes accessed | tf_op | source)
XLA Modules:
  0.0 114.1 jit_solution(3709308402546275231)
XLA Ops:
  0.6 0.8 reshape.27
  1.4 0.8 reshape.26
  2.2 0.0 copy-start
  2.2 0.7 fusion.4
  2.9 0.7 pad_add_fusion
  3.6 0.7 pad_add_fusion.1
  4.3 0.7 concatenate.21
  5.0 0.7 concatenate.22
  5.7 0.7 concatenate.23.idx
  6.3 0.0 copy-done
  6.3 29.7 %gather_rows.1 = (bf16[448,512]{1,0:T(8,128)(2,1)}, bf16[2,4,4,4,16,256]{5,4,3,2,1,0:T(8,128)(2,1)}, bf16[2,4,4,4,16,256]{5,4,3,2,1,0:T(8,128)(2,1)}) custom-call(bf16[128,512]{1,0:T(8,128)(2,1)} %nodes.3, s32[1,320]{1,0:T(1,128)} %copy-done), custom_call_target="tpu_custom_call" | custom-call | tf_op jit(solution)/shard_map/gather_rows/pallas_call | solution.py:192
  36.0 21.9 %layer.1 = (bf16[128,512]{1,0:T(8,128)(2,1)}, bf16[768,512]{1,0:T(8,128)(2,1)}, bf16[256,512]{1,0:T(8,128)(2,1)}, bf16[768,512]{1,0:T(8,128)(2,1)}, bf16[256,512...) custom-call(bf16[128,512]{1,0:T(8,128)(2,1)} %nodes.3, ...), custom_call_target="tpu_custom_call" | custom-call | tf_op jit(solution)/shard_map/layer/pallas_call | solution.py:445
  57.9 48.9 %reduce_all.1 = (f32[48,512]{1,0:T(8,128)}, f32[16,512]{1,0:T(8,128)}, f32[32,512]{1,0:T(8,128)}, f32[16,512]{1,0:T(8,128)}, bf16[128,512]{1,0:T(8,128)(2,1)}) custom-call(bf16[2,2,4,4,176,256]{5,4,3,2,1,0:T(8,128)(2,1)} %get-tuple-element.33.table, bf16[320,512]{1,0:T(8,128)(2,1)} %get-tuple-element.34.halo, f32[128,512]{1,0:T(8,128)} %get-tuple-element.35.own, ...), custom_call_target="tpu_custom_call" | custom-call | tf_op jit(solution)/shard_map/reduce_all/pallas_call | solution.py:683
  106.8 1.6 %copy.33 = bf16[128,512]{1,0:T(8,128)(2,1)} copy(bf16[128,512]{1,0:T(8,128)(2,1)} %get-tuple-element.57) | data formatting | bytes 262144
  108.4 1.5 %copy.34 = f32[48,512]{1,0:T(8,128)} copy(f32[48,512]{1,0:T(8,128)} %get-tuple-element.60) | data formatting | bytes 196608
  109.9 1.4 %copy.35 = f32[16,512]{1,0:T(8,128)} copy(f32[16,512]{1,0:T(8,128)} %get-tuple-element.61) | data formatting | bytes 65536
  111.3 1.5 %copy.36 = f32[32,512]{1,0:T(8,128)} copy(f32[32,512]{1,0:T(8,128)} %get-tuple-element.62) | data formatting | bytes 131072
  112.8 1.4 %copy.37 = f32[16,512]{1,0:T(8,128)} copy(f32[16,512]{1,0:T(8,128)} %get-tuple-element.63) | data formatting | bytes 65536
  (3 shorter events, 0.0 us)
Async XLA Ops:
  2.2 4.2 %copy-start = (s32[1,320]{1,0:T(1,128)}, s32[1,320]{1,0:T(1,128)S(1)}, u32[]{:S(2)}) copy-start(s32[1,320]{1,0:T(1,128)S(1)} %constant_dynamic-update-slice_fusion.lists) | copy-start | bytes 3844

commit v2 on v0

v2 whole, which is shorter than its diff:
```python
import functools
import math
from types import SimpleNamespace

import jax
import jax.numpy as jnp
from jax import lax
from jax.experimental import pallas as pl
from jax.experimental.pallas import tpu as pltpu
from jax.sharding import PartitionSpec as P

COARSE_DEV = 8
F32 = jnp.float32
BF16 = jnp.bfloat16
MESH = pl.DeviceIdType.MESH
EPS = 1e-05
TILE = 256
VMEM_BYTES = 56 * 1024 * 1024


def dot(left, right):
    return jnp.dot(left, right, preferred_element_type=F32)


def dot_tn(left, right):
    return lax.dot_general(left, right, (((0,), (0,)), ((), ())), preferred_element_type=F32)


def dot_nt(left, right):
    return lax.dot_general(left, right, (((1,), (1,)), ((), ())), preferred_element_type=F32)


def split(values):
    high = values.astype(BF16)
    return high, (values - high.astype(F32)).astype(BF16)


def marks(hits):
    return jnp.where(hits, 1.0, 0.0).astype(BF16)


class Place:
    def __init__(self, side, depth):
        self.p = lax.axis_index("patch")
        self.z = lax.axis_index("sub")
        self.side, self.depth = side, depth
        self.core = lax.rem(self.p, 2)
        self.x = lax.rem(lax.div(self.p, 2), side)
        self.y = lax.div(self.p, 2 * side)
        self.patches = 2 * side * side

    def at(self, y, x, core):
        return (y * self.side + x) * 2 + core

    def along_x(self, by):
        return (self.at(self.y, lax.rem(self.x + by, self.side), self.core), self.z)

    def along_y(self, by):
        return (self.at(lax.rem(self.y + by, self.side), self.x, self.core), self.z)

    def along_z(self, by):
        return (self.p, lax.rem(self.z + by, self.depth))

    def other_core(self):
        return (self.at(self.y, self.x, 1 - self.core), self.z)

    def next_patch(self):
        return (lax.rem(self.p + 1, self.patches), self.z)

    def previous_patch(self):
        return (lax.rem(self.p + self.patches - 1, self.patches), self.z)

    def greet(self):
        peers = [self.along_x(by) for by in range(1, self.side)]
        peers += [self.along_y(by) for by in range(1, self.side)]
        peers += [self.along_z(by) for by in range(1, self.depth)]
        peers += [self.other_core(), self.next_patch(), self.previous_patch()]
        barrier = pltpu.get_barrier_semaphore()
        for peer in peers:
            pl.semaphore_signal(barrier, inc=1, device_id=peer, device_id_type=MESH)
        pl.semaphore_wait(barrier, len(peers))


def remote(source, target, sent, landed, peer):
    return pltpu.make_async_remote_copy(
        src_ref=source,
        dst_ref=target,
        send_sem=sent,
        recv_sem=landed,
        device_id=peer,
        device_id_type=MESH,
    )


def send(source, target, sent, landed, peer):
    copy = remote(source, target, sent, landed, peer)
    copy.start()
    return copy


def norm_rows(values):
    centered = values - jnp.mean(values, axis=-1, keepdims=True)
    inverse = lax.rsqrt(jnp.mean(centered * centered, axis=-1, keepdims=True) + EPS)
    return centered * inverse, inverse


def norm_back(normed, inverse, upstream):
    mean_grad = jnp.mean(upstream, axis=-1, keepdims=True)
    mean_prod = jnp.mean(upstream * normed, axis=-1, keepdims=True)
    return (upstream - mean_grad - normed * mean_prod) * inverse


def silu_and_slope(values):
    sigma = 0.5 + 0.5 * jnp.tanh(0.5 * values)
    active = values * sigma
    return active, sigma + active * (1.0 - sigma)


def coarse_spot(side, depth, coarse):
    block, row = coarse // COARSE_DEV, coarse % COARSE_DEV
    patch, z = block // depth, block % depth
    core, x, y = patch % 2, patch // 2 % side, patch // (2 * side)
    half = depth // 2
    lower = z < half
    major, minor = jnp.where(lower, y, x), jnp.where(lower, x, y)
    place = ((core * side + major) * side + minor) * half + z % half
    return 16 * (place + jnp.where(lower, 0, 2 * side * side * half)) + row


class Sum:
    def __init__(self, me, refs, name):
        self.me, self.side = me, me.side
        for key, ref in vars(refs).items():
            if key.startswith(name + "_"):
                setattr(self, key[len(name) + 1 :], ref)
        self.majors, self.minors = (me.x, me.y), (me.y, me.x)

    def put(self, patch, start, values):
        side, half = self.side, self.table.shape[-1]
        core, x, y = patch % 2, patch // 2 % side, patch // (2 * side)
        values = values.astype(BF16)
        rows = pl.ds(start, values.shape[0])
        self.table[core, 0, x, y, rows, :] = values[:, :half]
        self.table[core, 1, y, x, rows, :] = values[:, half:]

    def put_all(self, start, values, patches, first=0):
        per = values.shape[0] // patches
        for k in range(patches):
            self.put(first + k, start, values[k * per : (k + 1) * per, :])

    def start(self):
        self.cores = []
        for part in (0, 1):
            source, target = self.table.at[1 - self.me.core, part], self.other.at[part]
            sems = self.core_sem.at[0, part], self.core_sem.at[1, part]
            self.cores.append(send(source, target, *sems, self.me.other_core()))

    def first(self):
        me, side = self.me, self.side
        self.firsts = []
        for copy in self.cores:
            copy.wait_recv()
        for by in [*range(1, side), 0]:
            for part in (0, 1):
                major = lax.rem(self.majors[part] + by, side)

                def add(minor, carry, part=part, major=major):
                    spot = (me.core, part, major, minor)
                    self.table[spot] = self.table[spot] + self.other[part, major, minor]
                    return carry

                lax.fori_loop(0, side, add, 0)
                if by:
                    peer = me.along_x(by) if part == 0 else me.along_y(by)
                    source, target = self.table.at[me.core, part, major], self.first_in.at[part, by - 1]
                    sems = self.first_sem.at[0, part, by - 1], self.first_sem.at[1, part, by - 1]
                    self.firsts.append(send(source, target, *sems, peer))

    def second(self):
        me, side = self.me, self.side
        self.seconds = []
        for copy in self.firsts:
            copy.wait_recv()
        for by in [*range(1, side), 0]:
            for part in (0, 1):
                minor = lax.rem(self.minors[part] + by, side)
                total = self.table[me.core, part, self.majors[part], minor].astype(F32)
                for k in range(side - 1):
                    total = total + self.first_in[part, k, minor].astype(F32)
                self.middle[part, minor] = total.astype(BF16)
                if by:
                    peer = me.along_y(by) if part == 0 else me.along_x(by)
                    source, target = self.middle.at[part, minor], self.second_in.at[part, by - 1]
                    sems = self.second_sem.at[0, part, by - 1], self.second_sem.at[1, part, by - 1]
                    self.seconds.append(send(source, target, *sems, peer))

    def patch_total(self):
        for copy in self.seconds:
            copy.wait_recv()
        sums = []
        for part in (0, 1):
            total = self.middle[part, self.minors[part]].astype(F32)
            for k in range(self.side - 1):
                total = total + self.second_in[part, k].astype(F32)
            sums.append(total)
        return sums

    def across(self, blocks):
        me, depth = self.me, self.me.depth
        per = self.z_out.shape[1]
        for k in range(depth * per):
            if k < len(blocks):
                self.z_out[k // per, k % per] = blocks[k].astype(BF16)
            else:
                self.z_out[k // per, k % per] = jnp.zeros(self.z_out.shape[2:], BF16)
        self.crossing = []
        for by in range(1, depth):
            peer = me.along_z(by)
            sems = self.z_sem.at[0, by - 1], self.z_sem.at[1, by - 1]
            self.crossing.append(send(self.z_out.at[peer[1]], self.z_in.at[by - 1], *sems, peer))

    def cross_total(self):
        for copy in self.crossing:
            copy.wait_recv()
        total = self.z_out[self.me.z].astype(F32)
        for k in range(self.me.depth - 1):
            total = total + self.z_in[k].astype(F32)
        return total

    def share(self, total):
        me = self.me
        self.shares[me.z] = total.astype(BF16)
        self.sharing = []
        for by in range(1, me.depth):
            mine = self.shares.at[me.z]
            sems = self.w_sem.at[0, by - 1], self.w_sem.at[1, by - 1]
            self.sharing.append(send(mine, mine, *sems, me.along_z(by)))

    def block(self, k):
        per = self.shares.shape[1]
        return self.shares[k // per, k % per].astype(F32)

    def wait_sends(self):
        for copy in self.cores + self.firsts + self.seconds + self.crossing + self.sharing:
            copy.wait_send()

    sharing = []


def sum_scratch(side, depth, rows, half, blocks):
    per = -(-blocks // depth)
    sem = pltpu.SemaphoreType.DMA
    return dict(
        table=pltpu.VMEM((2, 2, side, side, rows, half), BF16),
        other=pltpu.VMEM((2, side, side, rows, half), BF16),
        first_in=pltpu.VMEM((2, side - 1, side, rows, half), BF16),
        middle=pltpu.VMEM((2, side, rows, half), BF16),
        second_in=pltpu.VMEM((2, side - 1, rows, half), BF16),
        z_out=pltpu.VMEM((depth, per, 16, half), BF16),
        z_in=pltpu.VMEM((depth - 1, per, 16, half), BF16),
        shares=pltpu.VMEM((depth, per, 16, half), BF16),
        core_sem=sem((2, 2)),
        first_sem=sem((2, 2, side - 1)),
        second_sem=sem((2, 2, side - 1)),
        z_sem=sem((2, depth - 1)),
        w_sem=sem((2, depth - 1)),
    )


def row_blocks(sums):
    return [part[at : at + 16, :] for at in range(0, sums[0].shape[0], 16) for part in sums]


def whole_kernel(side, depth, names, loaded, *all_refs):
    refs = SimpleNamespace(**dict(zip(names, all_refs)))
    me = Place(side, depth)
    nodes, ext, low, high, rows = refs.nodes, refs.ext, refs.low, refs.high, refs.rows
    idx, cols, lists = refs.idx, refs.cols, refs.lists
    count, width = nodes.shape
    half = depth // 2
    columns = width // 2
    hb = refs.sub_list.shape[1]
    fine_count = refs.fine.shape[0]
    long_count = refs.longs.shape[0]
    ext_rows = ext.shape[0]
    patches = 2 * side * side
    fine_tiles = fine_count // TILE
    long_tile = fine_count

    loads = SimpleNamespace()
    for number, name in enumerate(loaded):
        local_copy = getattr(refs, "v_" + name)
        copy = pltpu.make_async_copy(getattr(refs, name), local_copy, refs.load_sem.at[number])
        copy.start()
        setattr(loads, name, copy)
    w1, w2, nw1, nw2 = refs.v_w1, refs.v_w2, refs.v_nw1, refs.v_nw2
    fine, longs, up_fine, up_long = refs.v_fine, refs.v_longs, refs.v_up_fine, refs.v_up_long

    first = nodes[0:16, :].astype(F32)[0:8, :]
    block = jnp.concatenate([first[:, :columns], first[:, columns:]], axis=0).astype(BF16)
    in_low = me.z < half
    z_low = lax.rem(me.z, half)

    @pl.when(in_low)
    def _():
        low[me.core, me.y, me.x, z_low] = block

    @pl.when(jnp.logical_not(in_low))
    def _():
        high[me.core, me.x, me.y, z_low] = block

    for k in range(depth):
        lists[0:1, k * hb : (k + 1) * hb] = refs.sub_list[k : k + 1, :]
    for k in range(2):
        lists[0:1, (depth + k) * hb : (depth + k + 1) * hb] = refs.patch_list[k : k + 1, :]
    picks = marks(lax.broadcasted_iota(jnp.int32, (count, lists.shape[1]), 0) == lists[...])
    rows[...] = dot_tn(picks, nodes[...]).astype(BF16).reshape(depth + 2, hb, width)

    me.greet()

    for by in range(1, depth):
        sems = refs.zs_sem.at[0, by - 1], refs.zs_sem.at[1, by - 1]

        @pl.when(in_low)
        def _():
            mine = low.at[me.core, me.y, me.x, z_low]
            send(mine, mine, *sems, me.along_z(by))

        @pl.when(jnp.logical_not(in_low))
        def _():
            mine = high.at[me.core, me.x, me.y, z_low]
            send(mine, mine, *sems, me.along_z(by))

    halo = []
    own_rows = pl.ds(pl.multiple_of(count + hb * me.z, hb), hb)
    for by in range(1, depth):
        peer = me.along_z(by)
        sems = refs.sub_sem.at[0, by - 1], refs.sub_sem.at[1, by - 1]
        halo.append(send(rows.at[peer[1]], ext.at[own_rows, :], *sems, peer))
    for k, peer in enumerate((me.next_patch(), me.previous_patch())):
        target = ext.at[pl.ds(count + hb * (depth + k), hb), :]
        sems = refs.pat_sem.at[0, k], refs.pat_sem.at[1, k]
        halo.append(send(rows.at[depth + k], target, *sems, peer))

    idx[...] = jnp.zeros_like(idx)
    spots = coarse_spot(side, depth, refs.long_send[...])
    for k in range(fine_count // 128):
        lanes = slice(128 * k, 128 * (k + 1))
        idx[0:1, lanes] = refs.fine_send[k : k + 1, :]
        idx[1:2, lanes] = refs.fine_recv[k : k + 1, :]
    for k in range(long_count // 128):
        lanes = slice(fine_count + 128 * k, fine_count + 128 * (k + 1))
        idx[0:1, lanes] = spots[k : k + 1, :]
        idx[1:2, lanes] = refs.long_recv[k : k + 1, :]
        idx[2:3, lanes] = refs.long_mask[k : k + 1, :]
        idx[3:4, lanes] = refs.long_send[k : k + 1, :]
    cols[...] = idx[...].T
    ext[0:count, :] = nodes[...]
    ext[own_rows, :] = rows[me.z]
    agg, ga, g1, g2 = refs.agg, refs.ga, refs.g1, refs.g2
    g_recv, g_ext, recv_proj = refs.g_recv, refs.g_ext, refs.recv_proj
    for ref in (agg, g1, g2, g_recv, g_ext):
        ref[...] = jnp.zeros_like(ref)

    loads.w1.wait()
    high_part, low_part = split(dot(nodes[...], w1[2 * width : 3 * width, :]))
    recv_proj[0:count, :] = high_part
    recv_proj[count : 2 * count, :] = low_part

    mine = low.at[0, 0, 0, 0]
    for by in range(1, depth):
        sems = refs.zs_sem.at[0, by - 1], refs.zs_sem.at[1, by - 1]
        remote(mine, mine, *sems, me.along_z(by)).wait()

    def spread(step, low_part, high_part):
        copies = []
        for by in range(1, side):
            along = (me.along_x(by), me.along_y(by))
            for k, part in enumerate((low_part, high_part)):
                sems = refs.ab_sem.at[0, step, k, by - 1], refs.ab_sem.at[1, step, k, by - 1]
                copies.append(send(part, part, *sems, along[(step + k) % 2]))
        return copies

    spreading = spread(0, low.at[me.core, me.y, me.x], high.at[me.core, me.x, me.y])

    slope, active, normed, inverse = refs.slope, refs.active, refs.normed, refs.inverse
    senders = refs.senders

    def recv_cols(base):
        lanes = lax.broadcasted_iota(jnp.int32, (TILE, 2 * count), 1)
        return marks(lax.rem(lanes, count) == cols[base : base + TILE, 1:2])

    def recv_rows(base, live):
        spots = lax.broadcasted_iota(jnp.int32, (count, TILE), 0)
        hits = spots == idx[1:2, base : base + TILE]
        if live:
            hits = jnp.logical_and(hits, idx[2:3, base : base + TILE] > 0)
        return marks(hits)

    def forward(base, edges, sender, rest, live):
        senders[base : base + TILE, :] = sender
        act, slopes = silu_and_slope(rest + dot(sender, w1[width : 2 * width, :]))
        act = act.astype(BF16)
        slope[base : base + TILE, :] = slopes
        active[base : base + TILE, :] = act
        unit, scale = norm_rows(dot(act, w2[...]))
        normed[base : base + TILE, :] = unit
        inverse[base : base + TILE, :] = jnp.broadcast_to(scale, (TILE, 128))
        if live is not None:
            unit = unit * live
        new = (edges.astype(F32) + unit).astype(BF16)
        agg[...] += dot(recv_rows(base, live is not None), new)
        return new

    def sender_free(base, edges):
        return dot(edges, w1[0:width, :]) + dot(recv_cols(base), recv_proj[...])

    loads.fine.wait()
    loads.w2.wait()
    for copy in halo:
        copy.wait_recv()
    for step in range(fine_tiles):
        base = step * TILE
        edges = fine[base : base + TILE, :]
        lanes = lax.broadcasted_iota(jnp.int32, (TILE, ext_rows), 1)
        picks = marks(lanes == cols[base : base + TILE, 0:1])
        sender = dot(picks, ext[...]).astype(BF16)
        refs.v_new_fine[base : base + TILE, :] = forward(
            base, edges, sender, sender_free(base, edges), None
        )
        if step == 0:
            for copy in spreading:
                copy.wait()
            spreading = spread(1, low.at[me.core, me.y], high.at[me.core, me.x])
    loads.longs.wait()
    edges = longs[...]
    rest = sender_free(long_tile, edges)
    for copy in spreading:
        copy.wait()
    spreading = []
    for k, part in enumerate((low.at[me.core], high.at[me.core])):
        sems = refs.cc_sem.at[0, k], refs.cc_sem.at[1, k]
        spreading.append(send(part, part, *sems, me.other_core()))
    for copy in spreading:
        copy.wait()

    spot = cols[long_tile : long_tile + long_count, 0:1]
    major_rows = math.prod(low.shape[2:-1])
    lanes = lax.broadcasted_iota(jnp.int32, (long_count, major_rows), 1)
    left = jnp.zeros((long_count, columns), F32)
    right = jnp.zeros((long_count, columns), F32)
    for number in range(4 * side):
        part = low if number < 2 * side else high
        piece = part[number // side % 2, number % side].reshape(major_rows, columns)
        shifted = spot - number * major_rows
        left += dot(marks(lanes == shifted), piece)
        right += dot(marks(lanes == shifted + 8), piece)
    sender = jnp.concatenate([left, right], axis=1).astype(BF16)
    live = cols[long_tile : long_tile + long_count, 2:3].astype(F32)
    refs.v_new_long[...] = forward(long_tile, edges, sender, rest, live)

    stores = []

    def store(source, target):
        copy = pltpu.make_async_copy(source, target, refs.store_sem.at[len(stores)])
        copy.start()
        stores.append(copy)

    store(refs.v_new_fine, refs.out_fine)
    store(refs.v_new_long, refs.out_long)

    loads.nw1.wait()
    loads.nw2.wait()
    loads.up_nodes.wait()
    node_rows = nodes[...]
    aggregate = agg[...].astype(BF16)
    node_first = dot(node_rows, nw1[0:width, :]) + dot(aggregate, nw1[width : 2 * width, :])
    node_active, node_slope = silu_and_slope(node_first)
    node_active = node_active.astype(BF16)
    node_normed, node_inverse = norm_rows(dot(node_active, nw2[...]))
    refs.out_node[...] = (node_rows.astype(F32) + node_normed).astype(BF16)
    upstream = refs.v_up_nodes[...].astype(F32)
    ngs = norm_back(node_normed, node_inverse, upstream).astype(BF16)
    ngf = (dot_nt(ngs, nw2[...]) * node_slope).astype(BF16)
    by_node = Sum(me, refs, "n")
    per = [ref.shape[0] // patches for ref in (w1, w2, nw1, nw2)]
    by_node.put_all(per[2], dot_tn(node_active, ngs), patches)
    by_node.put_all(0, dot_tn(node_rows, ngf), patches // 2)
    by_node.put_all(0, dot_tn(aggregate, ngf), patches // 2, patches // 2)
    by_node.start()
    local = refs.local
    local[...] = upstream + dot_nt(ngf, nw1[0:width, :])
    high_part, low_part = split(dot_nt(ngf, nw1[width : 2 * width, :]))
    ga[0:count, :] = high_part
    ga[count : 2 * count, :] = low_part

    def backward(base, edges, upstream_rows, live):
        pulled = dot(recv_cols(base), ga[...])
        if live is not None:
            pulled = pulled * live
        egn = upstream_rows.astype(F32) + pulled
        egs = norm_back(normed[base : base + TILE, :], inverse[base : base + TILE, 0:1], egn)
        if live is not None:
            egs = egs * live
        egs = egs.astype(BF16)
        egf = (dot_nt(egs, w2[...]) * slope[base : base + TILE, :]).astype(BF16)
        g2[...] += dot_tn(active[base : base + TILE, :], egs)
        g1[0:width, :] += dot_tn(edges, egf)
        g1[width : 2 * width, :] += dot_tn(senders[base : base + TILE, :], egf)
        g_recv[...] += dot(recv_rows(base, False), egf)
        return egf, (egn + dot_nt(egf, w1[0:width, :])).astype(BF16)

    loads.up_long.wait()
    egf, grad = backward(long_tile, longs[...], up_long[...], live)
    refs.v_gl[...] = grad
    store(refs.v_gl, refs.out_gl)
    by_coarse = Sum(me, refs, "c")
    coarse_rows = COARSE_DEV * depth
    sources = idx[3:4, long_tile : long_tile + long_count]
    for patch in range(0, patches, 4):
        spots = lax.broadcasted_iota(jnp.int32, (4 * coarse_rows, long_count), 0)
        sums = dot(marks(spots + patch * coarse_rows == sources), egf)
        by_coarse.put_all(0, sums, 4, patch)
    by_coarse.start()
    by_node.first()

    loads.up_fine.wait()
    for step in range(fine_tiles):
        base = step * TILE
        egf, grad = backward(base, fine[base : base + TILE, :], up_fine[base : base + TILE, :], None)
        refs.v_gf[base : base + TILE, :] = grad
        spots = lax.broadcasted_iota(jnp.int32, (ext_rows, TILE), 0)
        g_ext[...] += dot(marks(spots == idx[0:1, base : base + TILE]), egf)
        if step == 0:
            by_coarse.first()
        if step == fine_tiles - 1:
            by_node.second()

    halo_out, back = refs.halo_out, refs.back
    halo_out[...] = g_ext[count:ext_rows, :].astype(BF16).reshape(depth + 2, hb, width)
    returns = []
    for by in range(1, depth):
        peer = me.along_z(by)
        sems = refs.rsub_sem.at[0, by - 1], refs.rsub_sem.at[1, by - 1]
        returns.append(send(halo_out.at[peer[1]], back.at[me.z], *sems, peer))
    for k, peer in enumerate((me.previous_patch(), me.next_patch())):
        sems = refs.rpat_sem.at[0, k], refs.rpat_sem.at[1, k]
        returns.append(send(halo_out.at[depth + k], back.at[depth + k], *sems, peer))
    back[me.z] = halo_out[me.z]

    high_part, low_part = split(g_recv[...])
    g1[2 * width : 3 * width, :] = dot_tn(node_rows, high_part) + dot_tn(node_rows, low_part)
    by_edge = Sum(me, refs, "e")
    by_edge.put_all(0, g1, patches)
    by_edge.put_all(per[0], g2, patches)
    by_edge.start()
    store(refs.v_gf, refs.out_gf)
    receiver_w = w1[2 * width : 3 * width, :]
    local[...] += dot_nt(high_part, receiver_w) + dot_nt(low_part, receiver_w)

    by_coarse.second()
    by_edge.first()
    by_node.across(row_blocks(by_node.patch_total()))
    sums = by_coarse.patch_total()
    by_coarse.across(
        [
            jnp.concatenate([part[8 * k : 8 * (k + 1), :] for part in sums], axis=0)
            for k in range(depth)
        ]
    )
    for copy in returns:
        copy.wait()
    picks = marks(lax.broadcasted_iota(jnp.int32, (count, lists.shape[1]), 0) == lists[...])
    sent = g_ext[0:count, :] + dot(picks, back[...].reshape((depth + 2) * hb, width))
    by_node.share(by_node.cross_total())
    by_edge.second()

    total = by_coarse.cross_total()[0]
    coarse = jnp.concatenate([total[0:8, :], total[8:16, :]], axis=1)
    sent = jnp.concatenate([sent[0:8, :] + coarse, sent[8:, :]], axis=0)
    high_part, low_part = split(sent)
    sender_w = w1[width : 2 * width, :]
    sent_grad = dot_nt(high_part, sender_w) + dot_nt(low_part, sender_w)
    refs.out_gn[...] = (local[...] + sent_grad).astype(BF16)

    by_edge.across(row_blocks(by_edge.patch_total()))
    by_edge.share(by_edge.cross_total())
    for group, outs in ((by_node, (refs.out_nw1, refs.out_nw2)), (by_edge, (refs.out_w1, refs.out_w2))):
        for copy in group.sharing:
            copy.wait_recv()
        at = 0
        for out in outs:
            for row in range(0, out.shape[0], 16):
                for part in (0, 1):
                    out[row : row + 16, part * columns : (part + 1) * columns] = group.block(at)
                    at += 1
    for group in (by_node, by_coarse, by_edge):
        group.wait_sends()
    for copy in halo:
        copy.wait_send()
    for copy in stores:
        copy.wait()


def whole(side, depth, arrays):
    shapes = SimpleNamespace(**{name: array.shape for name, array in arrays.items()})
    loaded = tuple(n for n in arrays if arrays[n].dtype == BF16 and n != "nodes")
    count, width = shapes.nodes
    half, columns = depth // 2, width // 2
    hb = shapes.sub_list[1]
    patches = 2 * side * side
    edges = shapes.fine[0] + shapes.longs[0]
    ext_rows = count + (depth + 2) * hb
    per = [dims[0] // patches for dims in (shapes.w1, shapes.w2, shapes.nw1, shapes.nw2)]
    sem = pltpu.SemaphoreType.DMA
    vmem = pl.BlockSpec(memory_space=pltpu.VMEM)
    any_space = pl.BlockSpec(memory_space=pl.ANY)

    outs = dict(
        out_node=(shapes.nodes, BF16),
        out_fine=(shapes.fine, BF16),
        out_long=(shapes.longs, BF16),
        out_gn=(shapes.nodes, BF16),
        out_gf=(shapes.fine, BF16),
        out_gl=(shapes.longs, BF16),
        out_w1=((per[0], width), F32),
        out_w2=((per[1], width), F32),
        out_nw1=((per[2], width), F32),
        out_nw2=((per[3], width), F32),
    )
    scratch = {"v_" + n: pltpu.VMEM(arrays[n].shape, BF16) for n in loaded}
    scratch |= dict(
        v_new_fine=pltpu.VMEM(shapes.fine, BF16),
        v_new_long=pltpu.VMEM(shapes.longs, BF16),
        v_gf=pltpu.VMEM(shapes.fine, BF16),
        v_gl=pltpu.VMEM(shapes.longs, BF16),
        load_sem=sem((len(loaded),)),
        store_sem=sem((4,)),
        ext=pltpu.VMEM((ext_rows, width), BF16),
        low=pltpu.VMEM((2, side, side, half, 16, columns), BF16),
        high=pltpu.VMEM((2, side, side, half, 16, columns), BF16),
        rows=pltpu.VMEM((depth + 2, hb, width), BF16),
        lists=pltpu.VMEM((1, (depth + 2) * hb), jnp.int32),
        idx=pltpu.VMEM((8, edges), jnp.int32),
        cols=pltpu.VMEM((edges, 8), jnp.int32),
        slope=pltpu.VMEM((edges, width), F32),
        active=pltpu.VMEM((edges, width), BF16),
        normed=pltpu.VMEM((edges, width), F32),
        inverse=pltpu.VMEM((edges, 128), F32),
        senders=pltpu.VMEM((edges, width), BF16),
        recv_proj=pltpu.VMEM((2 * count, width), BF16),
        agg=pltpu.VMEM((count, width), F32),
        ga=pltpu.VMEM((2 * count, width), BF16),
        g1=pltpu.VMEM(shapes.w1, F32),
        g2=pltpu.VMEM(shapes.w2, F32),
        g_recv=pltpu.VMEM((count, width), F32),
        g_ext=pltpu.VMEM((ext_rows, width), F32),
        local=pltpu.VMEM((count, width), F32),
        halo_out=pltpu.VMEM((depth + 2, hb, width), BF16),
        back=pltpu.VMEM((depth + 2, hb, width), BF16),
        zs_sem=sem((2, depth - 1)),
        sub_sem=sem((2, depth - 1)),
        pat_sem=sem((2, 2)),
        ab_sem=sem((2, 2, 2, side - 1)),
        cc_sem=sem((2, 2)),
        rsub_sem=sem((2, depth - 1)),
        rpat_sem=sem((2, 2)),
    )
    groups = dict(
        n=(per[2] + per[3], 2 * (per[2] + per[3]) // 16),
        c=(COARSE_DEV * depth, depth),
        e=(per[0] + per[1], 2 * (per[0] + per[1]) // 16),
    )
    for key, (rows, blocks) in groups.items():
        for field, kind in sum_scratch(side, depth, rows, columns, blocks).items():
            scratch[key + "_" + field] = kind
    names = (*arrays, *outs, *scratch)
    return pl.pallas_call(
        functools.partial(whole_kernel, side, depth, names, loaded),
        out_shape=tuple(jax.ShapeDtypeStruct(dims, kind) for dims, kind in outs.values()),
        in_specs=[any_space if n in loaded else vmem for n in arrays],
        out_specs=tuple(
            any_space if kind == BF16 and dims[0] > count else vmem for dims, kind in outs.values()
        ),
        scratch_shapes=list(scratch.values()),
        compiler_params=pltpu.CompilerParams(
            collective_id=0, has_side_effects=True, vmem_limit_bytes=VMEM_BYTES
        ),
        name="whole_layer",
    )(*arrays.values())


def hand_over_kernel(number, *refs):
    held, sems = refs[2 * number : 3 * number], refs[3 * number]
    arriving = [
        pltpu.make_async_copy(refs[k], held[k], sems.at[0, k]) for k in range(number)
    ]
    leaving = [
        pltpu.make_async_copy(held[k], refs[number + k], sems.at[1, k]) for k in range(number)
    ]
    for copy in arriving:
        copy.start()
    for k in range(number):
        arriving[k].wait()
        leaving[k].start()
    for copy in leaving:
        copy.wait()


def hand_over(results):
    number = len(results)
    any_space = pl.BlockSpec(memory_space=pl.ANY)
    return pl.pallas_call(
        functools.partial(hand_over_kernel, number),
        out_shape=tuple(jax.ShapeDtypeStruct(r.shape, r.dtype) for r in results),
        in_specs=[any_space] * number,
        out_specs=(any_space,) * number,
        scratch_shapes=[pltpu.VMEM(r.shape, r.dtype) for r in results]
        + [pltpu.SemaphoreType.DMA((2, number))],
        compiler_params=pltpu.CompilerParams(vmem_limit_bytes=VMEM_BYTES),
        name="hand_over",
    )(*results)


def per_device(
    side,
    depth,
    nodes,
    fine_edges,
    long_edges,
    fine_send,
    fine_recv,
    long_send,
    long_recv,
    long_mask,
    sub_list,
    patch_list,
    edge_w1,
    edge_w2,
    node_w1,
    node_w2,
    upstream_nodes,
    upstream_fine,
    upstream_long,
):
    def tiles(values):
        return values.reshape(-1, 128)

    arrays = dict(
        nodes=nodes,
        fine_send=tiles(fine_send),
        fine_recv=tiles(fine_recv),
        long_send=tiles(long_send),
        long_recv=tiles(long_recv),
        long_mask=tiles(long_mask),
        sub_list=sub_list,
        patch_list=patch_list,
        w1=edge_w1,
        fine=fine_edges,
        w2=edge_w2,
        longs=long_edges,
        nw1=node_w1,
        nw2=node_w2,
        up_nodes=upstream_nodes,
        up_long=upstream_long,
        up_fine=upstream_fine,
    )
    return hand_over(whole(side, depth, arrays))


def solution(mesh):
    side = math.isqrt(mesh.shape["patch"] // 2)
    depth = mesh.shape["sub"]
    rows = P(("patch", "sub"), None)
    flat = P(("patch", "sub"))
    return jax.shard_map(
        functools.partial(per_device, side, depth),
        mesh=mesh,
        in_specs=(rows,) * 3 + (flat,) * 5 + (rows,) * 2 + (P(),) * 4 + (rows,) * 3,
        out_specs=(rows,) * 6 + (P("patch", None),) * 4,
        check_vma=False,
    )
```

time: 1940 us -> 80.4 us (0.04)
  waiting for transfers between devices: 1710 us -> 0 us
  Pallas kernels: 0 us -> 79.4 us
  other arithmetic: 70.2 us -> 0 us
  local copies, waits for them, and re-layouts: 69 us -> 0 us
  matrix products: 37 us -> 0 us
  blocking collectives: 27.9 us -> 0 us
    reduce_scatter x6 -> x0, waiting for transfers between devices: 1570 us -> none  [the longest x1 1260 us: per_device(): lax.psum_scatter(coarse_table, ('patch', 'sub'), scatter_dimension=0, til...]
    pallas_call x0 -> x2, Pallas kernels: none -> 79.4 us  [the longest x1 76.6 us: whole(): pl.pallas_call(functools.partial(whole_kernel, side, depth, names, loaded...]
    all_gather x2 -> x0, waiting for transfers between devices: 68.9 us -> none  [the longest x1 68.9 us: per_device(): lax.all_gather(nodes[:COARSE_DEV], ('patch', 'sub'), axis=0, tiled=True)]
    psum x1 -> x0, waiting for transfers between devices: 65.5 us -> none  [per_device(): lax.psum(shares[0].astype(jnp.bfloat16), 'sub').astype(jnp.float32)]
    dot_general x12 -> x0, matrix products: 37 us -> none  [the longest x4 16.1 us: contract(): lax.dot_general(left, right, (((0,), (0,)), ((), ())), preferred_element_...]
    scatter-add x5 -> x0, other arithmetic: 31.3 us -> none  [the longest x1 7.6 us: per_device(): jax.ops.segment_sum(sender_grad[:fine_count], fine_send, num_segments=ext...]
    gather x14 -> x0, local copies, waits for them, and re-layouts: 29.6 us -> none  [the longest x2 7.82 us: layer_pass(): jnp.take(grad_aggregate, recv_all, axis=0)]
    all_gather x1 -> x0, blocking collectives: 27.9 us -> none  [per_device(): group_lists = lax.all_gather(sub_list, 'sub', axis=0, tiled=True)]
  transfers between devices with their start and end apart: 13 -> 0, of which waited for: 8 -> 0; matrix products, arithmetic and copies ran while one was open for 7% -> 0% of each run, Pallas kernels for 0% -> 0%
where the time goes in v2:
time: 80.4 us; the launch traced here: 80.2 us
  Pallas kernels  79.4 us (99%)
  between operations  0.82 us (1%)
    pallas_call x1, Pallas kernels, whole(): pl.pallas_call(functools.partial(whole_kernel, side, depth, names, loaded...  76.6 us
    pallas_call x1, Pallas kernels, hand_over(): pl.pallas_call(functools.partial(hand_over_kernel, number), out_shape=tup...  2.81 us

profile of v2, /device:TPU:32, one launch (start us, length us, event | category | flops | bytes accessed | tf_op | source)
XLA Modules:
  0.0 80.2 jit_solution(8263951390671424173)
XLA Ops:
  0.6 76.6 %whole_layer.1 = (bf16[128,512]{1,0:T(8,128)(2,1)}, bf16[768,512]{1,0:T(8,128)(2,1)}, bf16[256,512]{1,0:T(8,128)(2,1)}, bf16[128,512]{1,0:T(8,128)(2,1)}, bf16[7...) custom-call(bf16[128,512]{1,0:T(8,128)(2,1)} %all_refs_0_.1, ...), custom_call_target="tpu_custom_call" | custom-call | tf_op jit(solution)/shard_map/whole_layer/pallas_call | solution.py:678
  77.3 2.8 %hand_over.1 = (bf16[128,512]{1,0:T(8,128)(2,1)}, bf16[768,512]{1,0:T(8,128)(2,1)}, bf16[256,512]{1,0:T(8,128)(2,1)}, bf16[128,512]{1,0:T(8,128)(2,1)}, bf16[768...) custom-call(bf16[128,512]{1,0:T(8,128)(2,1)} %get-tuple-element.20.r, ...), custom_call_target="tpu_custom_call" | custom-call | tf_op jit(solution)/shard_map/hand_over/pallas_call | solution.py:713

commit v3 on v2

--- a/solution.py
+++ b/solution.py
@@ -75,10 +75,15 @@
         peers += [self.along_y(by) for by in range(1, self.side)]
         peers += [self.along_z(by) for by in range(1, self.depth)]
         peers += [self.other_core(), self.next_patch(), self.previous_patch()]
-        barrier = pltpu.get_barrier_semaphore()
         for peer in peers:
-            pl.semaphore_signal(barrier, inc=1, device_id=peer, device_id_type=MESH)
-        pl.semaphore_wait(barrier, len(peers))
+            pl.semaphore_signal(
+                pltpu.get_barrier_semaphore(), inc=1, device_id=peer, device_id_type=MESH
+            )
+        return len(peers)
+
+
+def far_first(peers):
+    return sorted(range(1, peers), key=lambda by: -min(by, peers - by))
 
 
 def remote(source, target, sent, landed, peer):
@@ -149,39 +154,36 @@
             self.put(first + k, start, values[k * per : (k + 1) * per, :])
 
     def start(self):
-        self.cores = []
-        for part in (0, 1):
-            source, target = self.table.at[1 - self.me.core, part], self.other.at[part]
-            sems = self.core_sem.at[0, part], self.core_sem.at[1, part]
-            self.cores.append(send(source, target, *sems, self.me.other_core()))
+        self.cores = {}
+        for by in [*far_first(self.side), 0]:
+            for part in (0, 1):
+                major = lax.rem(self.majors[part] + by, self.side)
+                source = self.table.at[1 - self.me.core, part, major]
+                sems = self.core_sem.at[0, part, by], self.core_sem.at[1, part, by]
+                copy = send(source, self.other.at[part, major], *sems, self.me.other_core())
+                self.cores[part, by] = copy
 
     def first(self):
-        me, side = self.me, self.side
+        me = self.me
         self.firsts = []
-        for copy in self.cores:
-            copy.wait_recv()
-        for by in [*range(1, side), 0]:
+        for by in [*far_first(self.side), 0]:
             for part in (0, 1):
-                major = lax.rem(self.majors[part] + by, side)
-
-                def add(minor, carry, part=part, major=major):
-                    spot = (me.core, part, major, minor)
-                    self.table[spot] = self.table[spot] + self.other[part, major, minor]
-                    return carry
-
-                lax.fori_loop(0, side, add, 0)
+                major = lax.rem(self.majors[part] + by, self.side)
+                self.cores[part, by].wait_recv()
+                spot = (me.core, part, major)
+                self.table[spot] = self.table[spot] + self.other[part, major]
                 if by:
                     peer = me.along_x(by) if part == 0 else me.along_y(by)
-                    source, target = self.table.at[me.core, part, major], self.first_in.at[part, by - 1]
+                    target = self.first_in.at[part, by - 1]
                     sems = self.first_sem.at[0, part, by - 1], self.first_sem.at[1, part, by - 1]
-                    self.firsts.append(send(source, target, *sems, peer))
+                    self.firsts.append(send(self.table.at[spot], target, *sems, peer))
 
     def second(self):
         me, side = self.me, self.side
         self.seconds = []
         for copy in self.firsts:
             copy.wait_recv()
-        for by in [*range(1, side), 0]:
+        for by in [*far_first(side), 0]:
             for part in (0, 1):
                 minor = lax.rem(self.minors[part] + by, side)
                 total = self.table[me.core, part, self.majors[part], minor].astype(F32)
@@ -214,7 +216,7 @@
             else:
                 self.z_out[k // per, k % per] = jnp.zeros(self.z_out.shape[2:], BF16)
         self.crossing = []
-        for by in range(1, depth):
+        for by in far_first(depth):
             peer = me.along_z(by)
             sems = self.z_sem.at[0, by - 1], self.z_sem.at[1, by - 1]
             self.crossing.append(send(self.z_out.at[peer[1]], self.z_in.at[by - 1], *sems, peer))
@@ -231,7 +233,7 @@
         me = self.me
         self.shares[me.z] = total.astype(BF16)
         self.sharing = []
-        for by in range(1, me.depth):
+        for by in far_first(me.depth):
             mine = self.shares.at[me.z]
             sems = self.w_sem.at[0, by - 1], self.w_sem.at[1, by - 1]
             self.sharing.append(send(mine, mine, *sems, me.along_z(by)))
@@ -241,7 +243,7 @@
         return self.shares[k // per, k % per].astype(F32)
 
     def wait_sends(self):
-        for copy in self.cores + self.firsts + self.seconds + self.crossing + self.sharing:
+        for copy in [*self.cores.values()] + self.firsts + self.seconds + self.crossing + self.sharing:
             copy.wait_send()
 
     sharing = []
@@ -259,7 +261,7 @@
         z_out=pltpu.VMEM((depth, per, 16, half), BF16),
         z_in=pltpu.VMEM((depth - 1, per, 16, half), BF16),
         shares=pltpu.VMEM((depth, per, 16, half), BF16),
-        core_sem=sem((2, 2)),
+        core_sem=sem((2, 2, side)),
         first_sem=sem((2, 2, side - 1)),
         second_sem=sem((2, 2, side - 1)),
         z_sem=sem((2, depth - 1)),
@@ -274,12 +276,12 @@
 def whole_kernel(side, depth, names, loaded, *all_refs):
     refs = SimpleNamespace(**dict(zip(names, all_refs)))
     me = Place(side, depth)
-    nodes, ext, low, high, rows = refs.nodes, refs.ext, refs.low, refs.high, refs.rows
+    nodes, ext, low, high, rows = refs.v_nodes, refs.ext, refs.low, refs.high, refs.rows
     idx, cols, lists = refs.idx, refs.cols, refs.lists
     count, width = nodes.shape
     half = depth // 2
     columns = width // 2
-    hb = refs.sub_list.shape[1]
+    hb = refs.v_sub_list.shape[1]
     fine_count = refs.fine.shape[0]
     long_count = refs.longs.shape[0]
     ext_rows = ext.shape[0]
@@ -287,15 +289,22 @@
     fine_tiles = fine_count // TILE
     long_tile = fine_count
 
+    greeted = me.greet()
     loads = SimpleNamespace()
-    for number, name in enumerate(loaded):
-        local_copy = getattr(refs, "v_" + name)
-        copy = pltpu.make_async_copy(getattr(refs, name), local_copy, refs.load_sem.at[number])
-        copy.start()
-        setattr(loads, name, copy)
+
+    def load(names):
+        for name in names:
+            source, target = getattr(refs, name), getattr(refs, "v_" + name)
+            sem = refs.load_sem.at[loaded.index(name)]
+            copy = pltpu.make_async_copy(source, target, sem)
+            copy.start()
+            setattr(loads, name, copy)
+
+    load(loaded[:8])
     w1, w2, nw1, nw2 = refs.v_w1, refs.v_w2, refs.v_nw1, refs.v_nw2
     fine, longs, up_fine, up_long = refs.v_fine, refs.v_longs, refs.v_up_fine, refs.v_up_long
 
+    loads.nodes.wait()
     first = nodes[0:16, :].astype(F32)[0:8, :]
     block = jnp.concatenate([first[:, :columns], first[:, columns:]], axis=0).astype(BF16)
     in_low = me.z < half
@@ -309,16 +318,8 @@
     def _():
         high[me.core, me.x, me.y, z_low] = block
 
-    for k in range(depth):
-        lists[0:1, k * hb : (k + 1) * hb] = refs.sub_list[k : k + 1, :]
-    for k in range(2):
-        lists[0:1, (depth + k) * hb : (depth + k + 1) * hb] = refs.patch_list[k : k + 1, :]
-    picks = marks(lax.broadcasted_iota(jnp.int32, (count, lists.shape[1]), 0) == lists[...])
-    rows[...] = dot_tn(picks, nodes[...]).astype(BF16).reshape(depth + 2, hb, width)
-
-    me.greet()
-
-    for by in range(1, depth):
+    pl.semaphore_wait(pltpu.get_barrier_semaphore(), greeted)
+    for by in far_first(depth):
         sems = refs.zs_sem.at[0, by - 1], refs.zs_sem.at[1, by - 1]
 
         @pl.when(in_low)
@@ -331,9 +332,56 @@
             mine = high.at[me.core, me.x, me.y, z_low]
             send(mine, mine, *sems, me.along_z(by))
 
+    load(loaded[8:11])
+    loads.sub_list.wait()
+    loads.patch_list.wait()
+    for k in range(depth):
+        lists[0:1, k * hb : (k + 1) * hb] = refs.v_sub_list[k : k + 1, :]
+    for k in range(2):
+        lists[0:1, (depth + k) * hb : (depth + k + 1) * hb] = refs.v_patch_list[k : k + 1, :]
+    picks = marks(lax.broadcasted_iota(jnp.int32, (count, lists.shape[1]), 0) == lists[...])
+    rows[...] = dot_tn(picks, nodes[...]).astype(BF16).reshape(depth + 2, hb, width)
+
+    own_rows = pl.ds(pl.multiple_of(count + hb * me.z, hb), hb)
+
+    idx[...] = jnp.zeros_like(idx)
+    for copy in (loads.fine_send, loads.fine_recv, loads.long_send, loads.long_recv, loads.long_mask):
+        copy.wait()
+    spots = coarse_spot(side, depth, refs.v_long_send[...])
+    for k in range(fine_count // 128):
+        lanes = slice(128 * k, 128 * (k + 1))
+        idx[0:1, lanes] = refs.v_fine_send[k : k + 1, :]
+        idx[1:2, lanes] = refs.v_fine_recv[k : k + 1, :]
+    for k in range(long_count // 128):
+        lanes = slice(fine_count + 128 * k, fine_count + 128 * (k + 1))
+        idx[0:1, lanes] = spots[k : k + 1, :]
+        idx[1:2, lanes] = refs.v_long_recv[k : k + 1, :]
+        idx[2:3, lanes] = refs.v_long_mask[k : k + 1, :]
+        idx[3:4, lanes] = refs.v_long_send[k : k + 1, :]
+    cols[...] = idx[...].T
+    ext[0:count, :] = nodes[...]
+    ext[own_rows, :] = rows[me.z]
+    agg, ga, g1 = refs.agg, refs.ga, refs.g1
+    g_ext, recv_proj = refs.g_ext, refs.recv_proj
+    agg[...] = jnp.zeros_like(agg)
+
+    mine = low.at[0, 0, 0, 0]
+    for by in range(1, depth):
+        sems = refs.zs_sem.at[0, by - 1], refs.zs_sem.at[1, by - 1]
+        remote(mine, mine, *sems, me.along_z(by)).wait()
+
+    def spread(step, low_part, high_part):
+        copies = []
+        for by in far_first(side):
+            along = (me.along_x(by), me.along_y(by))
+            for k, part in enumerate((low_part, high_part)):
+                sems = refs.ab_sem.at[0, step, k, by - 1], refs.ab_sem.at[1, step, k, by - 1]
+                copies.append(send(part, part, *sems, along[(step + k) % 2]))
+        return copies
+
+    spreading = spread(0, low.at[me.core, me.y, me.x], high.at[me.core, me.x, me.y])
     halo = []
-    own_rows = pl.ds(pl.multiple_of(count + hb * me.z, hb), hb)
-    for by in range(1, depth):
+    for by in far_first(depth):
         peer = me.along_z(by)
         sems = refs.sub_sem.at[0, by - 1], refs.sub_sem.at[1, by - 1]
         halo.append(send(rows.at[peer[1]], ext.at[own_rows, :], *sems, peer))
@@ -342,46 +390,11 @@
         sems = refs.pat_sem.at[0, k], refs.pat_sem.at[1, k]
         halo.append(send(rows.at[depth + k], target, *sems, peer))
 
-    idx[...] = jnp.zeros_like(idx)
-    spots = coarse_spot(side, depth, refs.long_send[...])
-    for k in range(fine_count // 128):
-        lanes = slice(128 * k, 128 * (k + 1))
-        idx[0:1, lanes] = refs.fine_send[k : k + 1, :]
-        idx[1:2, lanes] = refs.fine_recv[k : k + 1, :]
-    for k in range(long_count // 128):
-        lanes = slice(fine_count + 128 * k, fine_count + 128 * (k + 1))
-        idx[0:1, lanes] = spots[k : k + 1, :]
-        idx[1:2, lanes] = refs.long_recv[k : k + 1, :]
-        idx[2:3, lanes] = refs.long_mask[k : k + 1, :]
-        idx[3:4, lanes] = refs.long_send[k : k + 1, :]
-    cols[...] = idx[...].T
-    ext[0:count, :] = nodes[...]
-    ext[own_rows, :] = rows[me.z]
-    agg, ga, g1, g2 = refs.agg, refs.ga, refs.g1, refs.g2
-    g_recv, g_ext, recv_proj = refs.g_recv, refs.g_ext, refs.recv_proj
-    for ref in (agg, g1, g2, g_recv, g_ext):
-        ref[...] = jnp.zeros_like(ref)
-
     loads.w1.wait()
     high_part, low_part = split(dot(nodes[...], w1[2 * width : 3 * width, :]))
     recv_proj[0:count, :] = high_part
     recv_proj[count : 2 * count, :] = low_part
-
-    mine = low.at[0, 0, 0, 0]
-    for by in range(1, depth):
-        sems = refs.zs_sem.at[0, by - 1], refs.zs_sem.at[1, by - 1]
-        remote(mine, mine, *sems, me.along_z(by)).wait()
-
-    def spread(step, low_part, high_part):
-        copies = []
-        for by in range(1, side):
-            along = (me.along_x(by), me.along_y(by))
-            for k, part in enumerate((low_part, high_part)):
-                sems = refs.ab_sem.at[0, step, k, by - 1], refs.ab_sem.at[1, step, k, by - 1]
-                copies.append(send(part, part, *sems, along[(step + k) % 2]))
-        return copies
-
-    spreading = spread(0, low.at[me.core, me.y, me.x], high.at[me.core, me.x, me.y])
+    load(loaded[11:])
 
     slope, active, normed, inverse = refs.slope, refs.active, refs.normed, refs.inverse
     senders = refs.senders
@@ -415,8 +428,20 @@
     def sender_free(base, edges):
         return dot(edges, w1[0:width, :]) + dot(recv_cols(base), recv_proj[...])
 
+    def pass_on(low_row, high_row):
+        copies = []
+        for k, (part, row) in enumerate(((low, low_row), (high, high_row))):
+            sems = refs.cc_sem.at[0, k, row], refs.cc_sem.at[1, k, row]
+            source = part.at[me.core, row]
+            copies.append(send(source, source, *sems, me.other_core()))
+        return copies
+
     loads.fine.wait()
     loads.w2.wait()
+    for copy in spreading:
+        copy.wait()
+    spreading = spread(1, low.at[me.core, me.y], high.at[me.core, me.x])
+    passing = pass_on(me.y, me.x)
     for copy in halo:
         copy.wait_recv()
     for step in range(fine_tiles):
@@ -428,34 +453,31 @@
         refs.v_new_fine[base : base + TILE, :] = forward(
             base, edges, sender, sender_free(base, edges), None
         )
-        if step == 0:
-            for copy in spreading:
-                copy.wait()
-            spreading = spread(1, low.at[me.core, me.y], high.at[me.core, me.x])
     loads.longs.wait()
     edges = longs[...]
     rest = sender_free(long_tile, edges)
-    for copy in spreading:
+    for k, by in enumerate(far_first(side)[::-1]):
+        for copy in spreading[2 * (side - 2 - k) : 2 * (side - 1 - k)]:
+            copy.wait()
+        passing += pass_on(lax.rem(me.y + side - by, side), lax.rem(me.x + side - by, side))
+
+    spot = cols[long_tile : long_tile + long_count, 0:1]
+    spots = jnp.concatenate([spot, spot + 8], axis=0)
+    core_rows = math.prod(low.shape[1:-1])
+    lanes = lax.broadcasted_iota(jnp.int32, (2 * long_count, core_rows), 1)
+
+    def coarse_rows_of(core):
+        halves = jnp.zeros((2 * long_count, columns), F32)
+        for k, part in enumerate((low, high)):
+            here = spots - (2 * k + core) * core_rows
+            halves += dot(marks(lanes == here), part[core].reshape(core_rows, columns))
+        return halves
+
+    halves = coarse_rows_of(me.core)
+    for copy in passing:
         copy.wait()
-    spreading = []
-    for k, part in enumerate((low.at[me.core], high.at[me.core])):
-        sems = refs.cc_sem.at[0, k], refs.cc_sem.at[1, k]
-        spreading.append(send(part, part, *sems, me.other_core()))
-    for copy in spreading:
-        copy.wait()
-
-    spot = cols[long_tile : long_tile + long_count, 0:1]
-    major_rows = math.prod(low.shape[2:-1])
-    lanes = lax.broadcasted_iota(jnp.int32, (long_count, major_rows), 1)
-    left = jnp.zeros((long_count, columns), F32)
-    right = jnp.zeros((long_count, columns), F32)
-    for number in range(4 * side):
-        part = low if number < 2 * side else high
-        piece = part[number // side % 2, number % side].reshape(major_rows, columns)
-        shifted = spot - number * major_rows
-        left += dot(marks(lanes == shifted), piece)
-        right += dot(marks(lanes == shifted + 8), piece)
-    sender = jnp.concatenate([left, right], axis=1).astype(BF16)
+    halves += coarse_rows_of(1 - me.core)
+    sender = jnp.concatenate([halves[:long_count, :], halves[long_count:, :]], axis=1).astype(BF16)
     live = cols[long_tile : long_tile + long_count, 2:3].astype(F32)
     refs.v_new_long[...] = forward(long_tile, edges, sender, rest, live)
 
@@ -466,8 +488,6 @@
         copy.start()
         stores.append(copy)
 
-    store(refs.v_new_fine, refs.out_fine)
-    store(refs.v_new_long, refs.out_long)
 
     loads.nw1.wait()
     loads.nw2.wait()
@@ -494,26 +514,29 @@
     ga[0:count, :] = high_part
     ga[count : 2 * count, :] = low_part
 
-    def backward(base, edges, upstream_rows, live):
+    egs_all, egf_all = refs.egs, refs.egf
+
+    def backward(base, upstream_rows, live):
         pulled = dot(recv_cols(base), ga[...])
         if live is not None:
             pulled = pulled * live
         egn = upstream_rows.astype(F32) + pulled
         egs = norm_back(normed[base : base + TILE, :], inverse[base : base + TILE, 0:1], egn)
+        normed[base : base + TILE, :] = egn
         if live is not None:
             egs = egs * live
         egs = egs.astype(BF16)
         egf = (dot_nt(egs, w2[...]) * slope[base : base + TILE, :]).astype(BF16)
-        g2[...] += dot_tn(active[base : base + TILE, :], egs)
-        g1[0:width, :] += dot_tn(edges, egf)
-        g1[width : 2 * width, :] += dot_tn(senders[base : base + TILE, :], egf)
-        g_recv[...] += dot(recv_rows(base, False), egf)
-        return egf, (egn + dot_nt(egf, w1[0:width, :])).astype(BF16)
+        egs_all[base : base + TILE, :] = egs
+        egf_all[base : base + TILE, :] = egf
+        return egf
+
+    def edge_grad(base):
+        egf = egf_all[base : base + TILE, :]
+        return (normed[base : base + TILE, :] + dot_nt(egf, w1[0:width, :])).astype(BF16)
 
     loads.up_long.wait()
-    egf, grad = backward(long_tile, longs[...], up_long[...], live)
-    refs.v_gl[...] = grad
-    store(refs.v_gl, refs.out_gl)
+    egf = backward(long_tile, up_long[...], live)
     by_coarse = Sum(me, refs, "c")
     coarse_rows = COARSE_DEV * depth
     sources = idx[3:4, long_tile : long_tile + long_count]
@@ -527,19 +550,26 @@
     loads.up_fine.wait()
     for step in range(fine_tiles):
         base = step * TILE
-        egf, grad = backward(base, fine[base : base + TILE, :], up_fine[base : base + TILE, :], None)
-        refs.v_gf[base : base + TILE, :] = grad
-        spots = lax.broadcasted_iota(jnp.int32, (ext_rows, TILE), 0)
-        g_ext[...] += dot(marks(spots == idx[0:1, base : base + TILE]), egf)
-        if step == 0:
-            by_coarse.first()
-        if step == fine_tiles - 1:
-            by_node.second()
-
+        backward(base, up_fine[base : base + TILE, :], None)
+    by_coarse.first()
+
+    by_edge = Sum(me, refs, "e")
+    by_edge.put_all(per[0], dot_tn(active[...], egs_all[...]), patches)
+    fine_egf, long_egf = egf_all[0:fine_count, :], egf_all[fine_count:, :]
+    spots = lax.broadcasted_iota(jnp.int32, (count, fine_count + long_count), 0)
+    high_part, low_part = split(dot(marks(spots == idx[1:2, :]), egf_all[...]))
+    g1[0:width, :] = dot_tn(fine[...], fine_egf) + dot_tn(longs[...], long_egf)
+    g1[width : 2 * width, :] = dot_tn(senders[...], egf_all[...])
+    g1[2 * width : 3 * width, :] = dot_tn(node_rows, high_part) + dot_tn(node_rows, low_part)
+    by_edge.put_all(0, g1, patches)
+    by_edge.start()
+
+    spots = lax.broadcasted_iota(jnp.int32, (ext_rows, fine_count), 0)
+    g_ext[...] = dot(marks(spots == idx[0:1, 0:fine_count]), fine_egf)
     halo_out, back = refs.halo_out, refs.back
     halo_out[...] = g_ext[count:ext_rows, :].astype(BF16).reshape(depth + 2, hb, width)
     returns = []
-    for by in range(1, depth):
+    for by in far_first(depth):
         peer = me.along_z(by)
         sems = refs.rsub_sem.at[0, by - 1], refs.rsub_sem.at[1, by - 1]
         returns.append(send(halo_out.at[peer[1]], back.at[me.z], *sems, peer))
@@ -548,19 +578,24 @@
         returns.append(send(halo_out.at[depth + k], back.at[depth + k], *sems, peer))
     back[me.z] = halo_out[me.z]
 
-    high_part, low_part = split(g_recv[...])
-    g1[2 * width : 3 * width, :] = dot_tn(node_rows, high_part) + dot_tn(node_rows, low_part)
-    by_edge = Sum(me, refs, "e")
-    by_edge.put_all(0, g1, patches)
-    by_edge.put_all(per[0], g2, patches)
-    by_edge.start()
-    store(refs.v_gf, refs.out_gf)
+    by_node.second()
     receiver_w = w1[2 * width : 3 * width, :]
     local[...] += dot_nt(high_part, receiver_w) + dot_nt(low_part, receiver_w)
-
+    by_edge.first()
+    store(refs.v_new_fine, refs.out_fine)
+    store(refs.v_new_long, refs.out_long)
+    for step in range(fine_tiles - 1):
+        base = step * TILE
+        refs.v_gf[base : base + TILE, :] = edge_grad(base)
+    by_node.across(row_blocks(by_node.patch_total()))
     by_coarse.second()
-    by_edge.first()
-    by_node.across(row_blocks(by_node.patch_total()))
+    base = fine_count - TILE
+    refs.v_gf[base : base + TILE, :] = edge_grad(base)
+    refs.v_gl[...] = edge_grad(long_tile)
+    store(refs.v_gf, refs.out_gf)
+    store(refs.v_gl, refs.out_gl)
+    by_edge.second()
+    by_node.share(by_node.cross_total())
     sums = by_coarse.patch_total()
     by_coarse.across(
         [
@@ -572,8 +607,7 @@
         copy.wait()
     picks = marks(lax.broadcasted_iota(jnp.int32, (count, lists.shape[1]), 0) == lists[...])
     sent = g_ext[0:count, :] + dot(picks, back[...].reshape((depth + 2) * hb, width))
-    by_node.share(by_node.cross_total())
-    by_edge.second()
+    by_edge.across(row_blocks(by_edge.patch_total()))
 
     total = by_coarse.cross_total()[0]
     coarse = jnp.concatenate([total[0:8, :], total[8:16, :]], axis=1)
@@ -583,7 +617,6 @@
     sent_grad = dot_nt(high_part, sender_w) + dot_nt(low_part, sender_w)
     refs.out_gn[...] = (local[...] + sent_grad).astype(BF16)
 
-    by_edge.across(row_blocks(by_edge.patch_total()))
     by_edge.share(by_edge.cross_total())
     for group, outs in ((by_node, (refs.out_nw1, refs.out_nw2)), (by_edge, (refs.out_w1, refs.out_w2))):
         for copy in group.sharing:
@@ -604,7 +637,7 @@
 
 def whole(side, depth, arrays):
     shapes = SimpleNamespace(**{name: array.shape for name, array in arrays.items()})
-    loaded = tuple(n for n in arrays if arrays[n].dtype == BF16 and n != "nodes")
+    loaded = tuple(arrays)
     count, width = shapes.nodes
     half, columns = depth // 2, width // 2
     hb = shapes.sub_list[1]
@@ -628,7 +661,7 @@
         out_nw1=((per[2], width), F32),
         out_nw2=((per[3], width), F32),
     )
-    scratch = {"v_" + n: pltpu.VMEM(arrays[n].shape, BF16) for n in loaded}
+    scratch = {"v_" + n: pltpu.VMEM(arrays[n].shape, arrays[n].dtype) for n in loaded}
     scratch |= dict(
         v_new_fine=pltpu.VMEM(shapes.fine, BF16),
         v_new_long=pltpu.VMEM(shapes.longs, BF16),
@@ -652,8 +685,8 @@
         agg=pltpu.VMEM((count, width), F32),
         ga=pltpu.VMEM((2 * count, width), BF16),
         g1=pltpu.VMEM(shapes.w1, F32),
-        g2=pltpu.VMEM(shapes.w2, F32),
-        g_recv=pltpu.VMEM((count, width), F32),
+        egs=pltpu.VMEM((edges, width), BF16),
+        egf=pltpu.VMEM((edges, width), BF16),
         g_ext=pltpu.VMEM((ext_rows, width), F32),
         local=pltpu.VMEM((count, width), F32),
         halo_out=pltpu.VMEM((depth + 2, hb, width), BF16),
@@ -662,7 +695,7 @@
         sub_sem=sem((2, depth - 1)),
         pat_sem=sem((2, 2)),
         ab_sem=sem((2, 2, 2, side - 1)),
-        cc_sem=sem((2, 2)),
+        cc_sem=sem((2, 2, side)),
         rsub_sem=sem((2, depth - 1)),
         rpat_sem=sem((2, 2)),
     )
@@ -678,7 +711,7 @@
     return pl.pallas_call(
         functools.partial(whole_kernel, side, depth, names, loaded),
         out_shape=tuple(jax.ShapeDtypeStruct(dims, kind) for dims, kind in outs.values()),
-        in_specs=[any_space if n in loaded else vmem for n in arrays],
+        in_specs=[any_space] * len(arrays),
         out_specs=tuple(
             any_space if kind == BF16 and dims[0] > count else vmem for dims, kind in outs.values()
         ),

time: 80.4 us -> 73.3 us (0.912)
  Pallas kernels: 79.4 us -> 72.4 us
    pallas_call x1, Pallas kernels: 76.6 us -> 69.6 us  [whole(): pl.pallas_call(functools.partial(whole_kernel, side, depth, names, loaded...]
where the time goes in v3:
time: 73.3 us; the launch traced here: 73.2 us
  Pallas kernels  72.4 us (99%)
  between operations  0.82 us (1%)
    pallas_call x1, Pallas kernels, whole(): pl.pallas_call(functools.partial(whole_kernel, side, depth, names, loaded...  69.6 us
    pallas_call x1, Pallas kernels, hand_over(): pl.pallas_call(functools.partial(hand_over_kernel, number), out_shape=tup...  2.81 us

profile of v3, /device:TPU:32, one launch (start us, length us, event | category | flops | bytes accessed | tf_op | source)
XLA Modules:
  0.0 73.2 jit_solution(1527140798904441588)
XLA Ops:
  0.6 69.6 %whole_layer.1 = (bf16[128,512]{1,0:T(8,128)(2,1)}, bf16[768,512]{1,0:T(8,128)(2,1)}, bf16[256,512]{1,0:T(8,128)(2,1)}, bf16[128,512]{1,0:T(8,128)(2,1)}, bf16[7...) custom-call(bf16[128,512]{1,0:T(8,128)(2,1)} %all_refs_0_.1, ...), custom_call_target="tpu_custom_call" | custom-call | tf_op jit(solution)/shard_map/whole_layer/pallas_call | solution.py:711
  70.2 2.8 %hand_over.1 = (bf16[128,512]{1,0:T(8,128)(2,1)}, bf16[768,512]{1,0:T(8,128)(2,1)}, bf16[256,512]{1,0:T(8,128)(2,1)}, bf16[128,512]{1,0:T(8,128)(2,1)}, bf16[768...) custom-call(bf16[128,512]{1,0:T(8,128)(2,1)} %get-tuple-element.20.r, ...), custom_call_target="tpu_custom_call" | custom-call | tf_op jit(solution)/shard_map/hand_over/pallas_call | solution.py:746

commit v4 on v3

--- a/solution.py
+++ b/solution.py
@@ -71,9 +71,9 @@
         return (lax.rem(self.p + self.patches - 1, self.patches), self.z)
 
     def greet(self):
-        peers = [self.along_x(by) for by in range(1, self.side)]
-        peers += [self.along_y(by) for by in range(1, self.side)]
-        peers += [self.along_z(by) for by in range(1, self.depth)]
+        peers = [self.along_z(by) for by in far_first(self.depth)]
+        peers += [self.along_x(by) for by in far_first(self.side)]
+        peers += [self.along_y(by) for by in far_first(self.side)]
         peers += [self.other_core(), self.next_patch(), self.previous_patch()]
         for peer in peers:
             pl.semaphore_signal(
@@ -153,23 +153,28 @@
         for k in range(patches):
             self.put(first + k, start, values[k * per : (k + 1) * per, :])
 
-    def start(self):
+    def start(self, in_pieces=False):
         self.cores = {}
+        for by in [*far_first(self.side), 0] if in_pieces else [None]:
+            for part in (0, 1):
+                source, target = self.table.at[1 - self.me.core, part], self.other.at[part]
+                if in_pieces:
+                    major = lax.rem(self.majors[part] + by, self.side)
+                    source, target = source.at[major], target.at[major]
+                sems = self.core_sem.at[0, part, by or 0], self.core_sem.at[1, part, by or 0]
+                self.cores[part, by] = send(source, target, *sems, self.me.other_core())
+
+    def first(self):
+        me = self.me
+        self.firsts = []
+        for part in (0, 1):
+            if (part, None) in self.cores:
+                self.cores[part, None].wait_recv()
         for by in [*far_first(self.side), 0]:
             for part in (0, 1):
                 major = lax.rem(self.majors[part] + by, self.side)
-                source = self.table.at[1 - self.me.core, part, major]
-                sems = self.core_sem.at[0, part, by], self.core_sem.at[1, part, by]
-                copy = send(source, self.other.at[part, major], *sems, self.me.other_core())
-                self.cores[part, by] = copy
-
-    def first(self):
-        me = self.me
-        self.firsts = []
-        for by in [*far_first(self.side), 0]:
-            for part in (0, 1):
-                major = lax.rem(self.majors[part] + by, self.side)
-                self.cores[part, by].wait_recv()
+                if (part, by) in self.cores:
+                    self.cores[part, by].wait_recv()
                 spot = (me.core, part, major)
                 self.table[spot] = self.table[spot] + self.other[part, major]
                 if by:
@@ -289,7 +294,6 @@
     fine_tiles = fine_count // TILE
     long_tile = fine_count
 
-    greeted = me.greet()
     loads = SimpleNamespace()
 
     def load(names):
@@ -300,7 +304,8 @@
             copy.start()
             setattr(loads, name, copy)
 
-    load(loaded[:8])
+    load(loaded[:1])
+    greeted = me.greet()
     w1, w2, nw1, nw2 = refs.v_w1, refs.v_w2, refs.v_nw1, refs.v_nw2
     fine, longs, up_fine, up_long = refs.v_fine, refs.v_longs, refs.v_up_fine, refs.v_up_long
 
@@ -332,7 +337,7 @@
             mine = high.at[me.core, me.x, me.y, z_low]
             send(mine, mine, *sems, me.along_z(by))
 
-    load(loaded[8:11])
+    load(loaded[1:11])
     loads.sub_list.wait()
     loads.patch_list.wait()
     for k in range(depth):
@@ -361,7 +366,7 @@
     cols[...] = idx[...].T
     ext[0:count, :] = nodes[...]
     ext[own_rows, :] = rows[me.z]
-    agg, ga, g1 = refs.agg, refs.ga, refs.g1
+    agg, ga = refs.agg, refs.ga
     g_ext, recv_proj = refs.g_ext, refs.recv_proj
     agg[...] = jnp.zeros_like(agg)
 
@@ -509,7 +514,6 @@
     by_node.put_all(0, dot_tn(aggregate, ngf), patches // 2, patches // 2)
     by_node.start()
     local = refs.local
-    local[...] = upstream + dot_nt(ngf, nw1[0:width, :])
     high_part, low_part = split(dot_nt(ngf, nw1[width : 2 * width, :]))
     ga[0:count, :] = high_part
     ga[count : 2 * count, :] = low_part
@@ -558,11 +562,14 @@
     fine_egf, long_egf = egf_all[0:fine_count, :], egf_all[fine_count:, :]
     spots = lax.broadcasted_iota(jnp.int32, (count, fine_count + long_count), 0)
     high_part, low_part = split(dot(marks(spots == idx[1:2, :]), egf_all[...]))
-    g1[0:width, :] = dot_tn(fine[...], fine_egf) + dot_tn(longs[...], long_egf)
-    g1[width : 2 * width, :] = dot_tn(senders[...], egf_all[...])
-    g1[2 * width : 3 * width, :] = dot_tn(node_rows, high_part) + dot_tn(node_rows, low_part)
-    by_edge.put_all(0, g1, patches)
-    by_edge.start()
+    grad_w1 = [
+        dot_tn(fine[...], fine_egf) + dot_tn(longs[...], long_egf),
+        dot_tn(senders[...], egf_all[...]),
+        dot_tn(node_rows, high_part) + dot_tn(node_rows, low_part),
+    ]
+    grad_w1 = jnp.concatenate([part.astype(BF16) for part in grad_w1], axis=0)
+    by_edge.put_all(0, grad_w1, patches)
+    by_edge.start(in_pieces=True)
 
     spots = lax.broadcasted_iota(jnp.int32, (ext_rows, fine_count), 0)
     g_ext[...] = dot(marks(spots == idx[0:1, 0:fine_count]), fine_egf)
@@ -580,7 +587,12 @@
 
     by_node.second()
     receiver_w = w1[2 * width : 3 * width, :]
-    local[...] += dot_nt(high_part, receiver_w) + dot_nt(low_part, receiver_w)
+    local[...] = (
+        upstream
+        + dot_nt(ngf, nw1[0:width, :])
+        + dot_nt(high_part, receiver_w)
+        + dot_nt(low_part, receiver_w)
+    )
     by_edge.first()
     store(refs.v_new_fine, refs.out_fine)
     store(refs.v_new_long, refs.out_long)
@@ -684,7 +696,6 @@
         recv_proj=pltpu.VMEM((2 * count, width), BF16),
         agg=pltpu.VMEM((count, width), F32),
         ga=pltpu.VMEM((2 * count, width), BF16),
-        g1=pltpu.VMEM(shapes.w1, F32),
         egs=pltpu.VMEM((edges, width), BF16),
         egf=pltpu.VMEM((edges, width), BF16),
         g_ext=pltpu.VMEM((ext_rows, width), F32),
@@ -724,16 +735,19 @@
 
 
 def hand_over_kernel(number, *refs):
-    held, sems = refs[2 * number : 3 * number], refs[3 * number]
-    arriving = [
-        pltpu.make_async_copy(refs[k], held[k], sems.at[0, k]) for k in range(number)
-    ]
-    leaving = [
-        pltpu.make_async_copy(held[k], refs[number + k], sems.at[1, k]) for k in range(number)
-    ]
-    for copy in arriving:
-        copy.start()
+    sems = refs[3 * number]
+    pieces = []
     for k in range(number):
+        source, target, held = refs[k], refs[number + k], refs[2 * number + k]
+        for row in range(0, source.shape[0], TILE):
+            rows = pl.ds(row, min(TILE, source.shape[0] - row))
+            pieces.append((source.at[rows, :], held.at[rows, :], target.at[rows, :]))
+    arriving, leaving = [], []
+    for k, (source, held, target) in enumerate(pieces):
+        arriving.append(pltpu.make_async_copy(source, held, sems.at[0, k]))
+        leaving.append(pltpu.make_async_copy(held, target, sems.at[1, k]))
+        arriving[k].start()
+    for k in range(len(pieces)):
         arriving[k].wait()
         leaving[k].start()
     for copy in leaving:
@@ -749,7 +763,7 @@
         in_specs=[any_space] * number,
         out_specs=(any_space,) * number,
         scratch_shapes=[pltpu.VMEM(r.shape, r.dtype) for r in results]
-        + [pltpu.SemaphoreType.DMA((2, number))],
+        + [pltpu.SemaphoreType.DMA((2, sum(-(-r.shape[0] // TILE) for r in results)))],
         compiler_params=pltpu.CompilerParams(vmem_limit_bytes=VMEM_BYTES),
         name="hand_over",
     )(*results)

time: 73.3 us -> 73 us (level)
  no operation moved by 1% of the time
where the time goes in v4:
time: 73 us; the launch traced here: 72.8 us
  Pallas kernels  72 us (99%)
  between operations  0.82 us (1%)
    pallas_call x1, Pallas kernels, whole(): pl.pallas_call(functools.partial(whole_kernel, side, depth, names, loaded...  69.3 us
    pallas_call x1, Pallas kernels, hand_over(): pl.pallas_call(functools.partial(hand_over_kernel, number), out_shape=tup...  2.69 us

profile of v4, /device:TPU:32, one launch (start us, length us, event | category | flops | bytes accessed | tf_op | source)
XLA Modules:
  0.0 72.8 jit_solution(16889716717673368255)
XLA Ops:
  0.6 69.3 %whole_layer.1 = (bf16[128,512]{1,0:T(8,128)(2,1)}, bf16[768,512]{1,0:T(8,128)(2,1)}, bf16[256,512]{1,0:T(8,128)(2,1)}, bf16[128,512]{1,0:T(8,128)(2,1)}, bf16[7...) custom-call(bf16[128,512]{1,0:T(8,128)(2,1)} %all_refs_0_.1, ...), custom_call_target="tpu_custom_call" | custom-call | tf_op jit(solution)/shard_map/whole_layer/pallas_call | solution.py:722
  70.0 2.7 %hand_over.1 = (bf16[128,512]{1,0:T(8,128)(2,1)}, bf16[768,512]{1,0:T(8,128)(2,1)}, bf16[256,512]{1,0:T(8,128)(2,1)}, bf16[128,512]{1,0:T(8,128)(2,1)}, bf16[768...) custom-call(bf16[128,512]{1,0:T(8,128)(2,1)} %get-tuple-element.20.r, ...), custom_call_target="tpu_custom_call" | custom-call | tf_op jit(solution)/shard_map/hand_over/pallas_call | solution.py:760
